TPU v7x, 256 devices: a whole 4x4x8 slice. The times are simulated.
256 devices in a mesh: group: 16 (over x, y_hi, core), dp: 16 (over y_lo, z).
Axes of the slice: x: 4, y: 4 (y_hi: 2, y_lo: 2; y = y_hi * 2 + y_lo), z: 8, core: 2. Of those that a mesh axis runs over, the one named last changes fastest.
Arguments:
- student: bfloat16 [32768, 1024], P(('group', 'dp')), may hold values from -6 to 6
- teacher: bfloat16 [32768, 4096], P(('group', 'dp')), may hold values from -6 to 6
- teacher_similarity: float32 [32768, 2048], P(('group', 'dp')), may hold values from -0.5 to 1, as said below
- projector: bfloat16 [1024, 4096], replicated, may hold values from -0.1875 to 0.1875
- hard_group: int32 [32768, 2], P(('group', 'dp')), may hold values from 0 to 15, all different within a row; in each aligned block of 128 rows (0 to 127, 128 to 255, ...) at most 24 rows name the same one
- hard_local: int32 [32768, 2], P(('group', 'dp')), may hold values from 0 to 127
- hard_count: int32 [32768], P(('group', 'dp')), may hold values from 1 to 2
- text_weight: float32 [32768], P(('group', 'dp')), may hold values from 0.5 to 13
Outputs:
- mean_loss: float32 [], replicated
- student_gradient: bfloat16 [32768, 1024], P(('group', 'dp'))
- projector_gradient: float32 [1024, 4096], P('group', 'dp')
Inputs may be any that keep to these rules, and one draw needn't show every extreme that they name: `hard_group`: A text's 2 entries name different groups. Among the 128 texts of one device (aligned blocks of 128 rows) no group is named more than 24 times, and some block names some group exactly 24 times. Symmetric inside each similarity set: for the set starting at text s, teacher_similarity[i, j - s] equals teacher_similarity[j, i - s]; a text's entry for itself is 1.
All inputs are finite; a program needn't handle non-finite values.
Results may differ from a plain program's by a relative error of at most 0.025.
Values may be sent and summed in bfloat16 or wider, within the bound.
A program may use at most 192 MiB of HBM per device.

v0:
```python
import jax
import jax.numpy as jnp
from jax import lax
from jax.sharding import PartitionSpec as P

HARD = 2


EPSILON = 1e-06
SOFTMAX_TEMP = 0.05
SIMILARITY_COEF = 200.0
HARD_WEIGHT = 20.0
LOSS_SCALE = 1024.0


def row_norms(values):
    return jnp.sqrt(jnp.sum(values * values, 1, keepdims=True) + EPSILON)


def local(
    student, teacher, teacher_similarity, projector, hard_group, hard_local, hard_count, text_weight
):
    row_count = student.shape[0]
    groups = lax.axis_size("group")
    columns = lax.axis_size("dp")
    set_count = row_count * columns
    slot_count = row_count * HARD // groups * 3 // 2
    position = lax.axis_index("dp")
    teacher_float = teacher.astype(jnp.float32)
    teacher_unit = (teacher_float / row_norms(teacher_float)).astype(jnp.bfloat16)
    projected = jnp.dot(student, projector, preferred_element_type=jnp.float32)
    norm_values = row_norms(projected)
    student_unit = (projected / norm_values).astype(jnp.bfloat16)
    unit_set = lax.all_gather(student_unit, "dp", axis=0, tiled=True)
    student_similarity = jnp.einsum(
        "rp,mp->rm", student_unit, unit_set, preferred_element_type=jnp.float32
    )
    own_index = position * row_count + jnp.arange(row_count, dtype=jnp.int32)
    off_diagonal = (jnp.arange(set_count, dtype=jnp.int32)[None, :] != own_index[:, None]).astype(
        jnp.float32
    )
    student_scaled = student_similarity / SOFTMAX_TEMP
    teacher_scaled = teacher_similarity / SOFTMAX_TEMP
    student_exp = jnp.exp(student_scaled) * off_diagonal
    teacher_exp = jnp.exp(teacher_scaled) * off_diagonal
    total_s = jnp.sum(student_exp, 1)
    total_t = jnp.sum(teacher_exp, 1)
    log_s = jnp.log(total_s)
    log_t = jnp.log(total_t)
    student_probability = student_exp / total_s[:, None]
    teacher_probability = teacher_exp / total_t[:, None]
    sim_difference = student_similarity - teacher_similarity
    sim_term = SIMILARITY_COEF / set_count * jnp.sum(sim_difference * sim_difference, 1)
    kl_term = jnp.sum(
        teacher_probability * (teacher_scaled - log_t[:, None] - (student_scaled - log_s[:, None])),
        1,
    )
    log_s_set, log_t_set, weight_set = (
        lax.all_gather(log_s, "dp", axis=0, tiled=True),
        lax.all_gather(log_t, "dp", axis=0, tiled=True),
        lax.all_gather(text_weight, "dp", axis=0, tiled=True),
    )
    student_column = jnp.exp(student_scaled - log_s_set[None, :]) * off_diagonal
    teacher_column = jnp.exp(teacher_scaled - log_t_set[None, :]) * off_diagonal
    row_scale = text_weight[:, None]
    column_scale = weight_set[None, :]
    pair_weight = (
        2.0 * SIMILARITY_COEF / set_count * sim_difference * (row_scale + column_scale)
        + (
            (student_probability - teacher_probability) * row_scale
            + (student_column - teacher_column) * column_scale
        )
        / SOFTMAX_TEMP
    ).astype(jnp.bfloat16)
    set_grad = jnp.dot(pair_weight, unit_set, preferred_element_type=jnp.float32)
    entry_group = hard_group.reshape(-1)
    entry_local = hard_local.reshape(-1)
    entry_count = jnp.repeat(hard_count, HARD)
    entry_scale = jnp.repeat(text_weight, HARD)
    entry_order = jnp.tile(jnp.arange(HARD, dtype=jnp.int32), row_count)
    group_hot = (entry_group[:, None] == jnp.arange(groups, dtype=jnp.int32)[None, :]).astype(
        jnp.int32
    )
    before = jnp.cumsum(group_hot, 0) - group_hot
    slot_rank = jnp.sum(before * group_hot, 1)
    slot_index = entry_group * slot_count + slot_rank
    slot_hot = slot_index[:, None] == jnp.arange(groups * slot_count, dtype=jnp.int32)[None, :]
    request = jnp.sum(jnp.where(slot_hot, entry_local[:, None], 0), 0).reshape(groups, slot_count)
    asked_rows = lax.all_to_all(request, "group", split_axis=0, concat_axis=0, tiled=True)
    picker = (
        asked_rows.reshape(-1)[:, None] == jnp.arange(row_count, dtype=jnp.int32)[None, :]
    ).astype(jnp.bfloat16)
    sent_unit = (
        jnp.dot(picker, student_unit, preferred_element_type=jnp.float32)
        .astype(jnp.bfloat16)
        .reshape(groups, slot_count, -1)
    )
    sent_teacher = (
        jnp.dot(picker, teacher_unit, preferred_element_type=jnp.float32)
        .astype(jnp.bfloat16)
        .reshape(groups, slot_count, -1)
    )
    got_unit, got_teacher = (
        lax.all_to_all(sent_unit, "group", split_axis=0, concat_axis=0, tiled=True),
        lax.all_to_all(sent_teacher, "group", split_axis=0, concat_axis=0, tiled=True),
    )
    slot_matrix = slot_hot.astype(jnp.bfloat16)
    neg_unit = jnp.dot(
        slot_matrix, got_unit.reshape(groups * slot_count, -1), preferred_element_type=jnp.float32
    )
    neg_teacher = jnp.dot(
        slot_matrix,
        got_teacher.reshape(groups * slot_count, -1),
        preferred_element_type=jnp.float32,
    )
    query_unit = jnp.repeat(student_unit, HARD, axis=0).astype(jnp.float32)
    query_teacher = jnp.repeat(teacher_unit, HARD, axis=0).astype(jnp.float32)
    student_hard = jnp.sum(query_unit * neg_unit, 1)
    teacher_hard = jnp.sum(query_teacher * neg_teacher, 1)
    validity = (entry_order < entry_count).astype(jnp.float32)
    weight = validity * HARD_WEIGHT / entry_count.astype(jnp.float32)
    hard_gap = student_hard - teacher_hard
    hard_term = jnp.sum((weight * hard_gap * hard_gap).reshape(row_count, HARD), 1)
    factor = 2.0 * entry_scale * weight * hard_gap
    own_hard = jnp.sum((factor[:, None] * neg_unit).reshape(row_count, HARD, -1), 1)
    returned_terms = (factor[:, None] * query_unit).astype(jnp.bfloat16)
    slotted = (
        jnp.dot(slot_matrix.T, returned_terms, preferred_element_type=jnp.float32)
        .astype(jnp.bfloat16)
        .reshape(groups, slot_count, -1)
    )
    arrived = lax.all_to_all(slotted, "group", split_axis=0, concat_axis=0, tiled=True)
    remote = jnp.dot(
        picker.T, arrived.reshape(groups * slot_count, -1), preferred_element_type=jnp.float32
    )
    own_teacher = teacher_unit.astype(jnp.float32)
    cos_term = 1.0 - jnp.sum(student_unit.astype(jnp.float32) * own_teacher, 1)
    local_loss = jnp.sum(text_weight * (cos_term + sim_term + kl_term + hard_term))
    loss_total = lax.psum(local_loss, ("group", "dp"))
    mean_loss = loss_total / (row_count * groups * columns)
    unit_gradient = LOSS_SCALE * (set_grad - row_scale * own_teacher + own_hard + remote)
    inner = jnp.sum(projected * unit_gradient, 1, keepdims=True)
    proj_gradient = (
        unit_gradient / norm_values - projected * inner / (norm_values * norm_values * norm_values)
    ).astype(jnp.bfloat16)
    student_gradient = jnp.einsum(
        "rp,dp->rd", proj_gradient, projector, preferred_element_type=jnp.float32
    ).astype(jnp.bfloat16)
    partial_weight = jnp.einsum(
        "rd,rp->dp", student, proj_gradient, preferred_element_type=jnp.float32
    )
    within = lax.psum_scatter(
        partial_weight.astype(jnp.bfloat16), "dp", scatter_dimension=1, tiled=True
    )
    projector_gradient = lax.psum_scatter(within, "group", scatter_dimension=0, tiled=True).astype(
        jnp.float32
    )
    return (mean_loss, student_gradient, projector_gradient)


def solution(mesh):
    return jax.shard_map(
        local,
        mesh=mesh,
        in_specs=(
            P(("group", "dp"), None),
            P(("group", "dp"), None),
            P(("group", "dp"), None),
            P(),
            P(("group", "dp"), None),
            P(("group", "dp"), None),
            P(("group", "dp")),
            P(("group", "dp")),
        ),
        out_specs=(P(), P(("group", "dp"), None), P("group", "dp")),
        check_vma=False,
    )
```

profile of v0, /device:TPU:1, one launch (start us, length us, event | category | flops | bytes accessed | tf_op | source)
XLA Modules:
  0.0 672.8 jit_solution(3884774772349315070)
XLA Ops:
  7.2 0.9 copy-done
  8.1 4.7 multiply_reduce_fusion.3
  12.9 0.3 fusion.2
  13.2 2.2 multiply_reduce_fusion.2
  15.5 0.1 eq.54
  15.7 0.1 reshape.143
  15.8 0.6 reduce-window.6
  16.4 0.2 slice_reduce_fusion
  16.8 0.1 broadcast_in_dim.27
  17.0 0.2 select_reduce_fusion
  17.3 15.2 %all_to_all.24 = s32[16,1,24]{2,1,0:T(1,128)S(1)} all-to-all(s32[16,1,24]{2,1,0:T(1,128)S(1)} %all_to_all.15), channel_id=1, replica_groups=mesh['group'=16,'dp'=16] {'group'}, dimensions={0} | all-to-all | bytes 3072 | tf_op jit(solution)/shard_map/all_to_all | solution.py:89
  32.5 0.5 broadcast.120
  33.0 0.7 reduce.5
  33.8 2.7 convolution_convert_fusion.1
  36.5 5.0 all-to-all-start.2
  41.5 2.7 convolution_convert_fusion.2
  44.2 195.0 %all-to-all-done.2 = bf16[16,24,4096]{2,1,0:T(8,128)(2,1)} async-done(((bf16[16,24,4096]{2,1,0:T(8,128)(2,1)}), bf16[16,24,4096]{2,1,0:T(8,128)(2,1)}, u32[]{:S(2)}, u32[]{:S(2)}) %all-to-all-start.2) | async-done | bytes 3145760 | tf_op jit(solution)/shard_map/all_to_all | solution.py:105
  239.2 4.7 all-to-all-start.1
  243.9 4.1 broadcast_in_dim.26
  248.0 6.1 convert_element_type.83
  254.0 5.9 broadcast_in_dim.30
  260.0 6.1 convert_element_type.87
  266.2 0.1 mul.209
  266.3 24.8 %all-gather = f32[16,1,128]{2,1,0:T(1,128)S(1)} all-gather(f32[1,1,128]{2,1,0:T(1,128)S(1)} %bitcast.53), channel_id=1, replica_groups=mesh['group'=16,'dp'=16] {'dp'}, dimensions={0}, use_global_device_ids=true | all-gather | bytes 8704 | tf_op jit(solution)/shard_map/all_gather | solution.py:61
  291.1 4.5 fusion.5
  295.7 6.6 multiply_reduce_fusion
  302.3 2.9 convolution_convert_fusion
  305.1 13.6 %all-to-all-start.3 = ((bf16[16,24,4096]{2,1,0:T(8,128)(2,1)}), bf16[16,24,4096]{2,1,0:T(8,128)(2,1)}, u32[]{:S(2)}, u32[]{:S(2)}) async-start(bf16[16,24,4096]{2,1,0:T(8,128)(2,1)} %bitcast.47), calls=%async_computation.3 | async-start | bytes 6291456 | tf_op jit(solution)/shard_map/all_to_all | solution.py:132
  318.7 4.7 broadcast_multiply_fusion
  323.4 5.8 reshape.149
  329.2 8.8 %reduce_sum.148 = f32[128,4096]{1,0:T(8,128)} reduce(f32[128,2,4096]{2,1,0:T(2,128)} %reshape.149, f32[]{:T(128)} %constant.14.clone.1), dimensions={1}, to_apply=%region_16.17 | reduce | flops 524288 | bytes 6291460 | tf_op jit(solution)/shard_map/reduce_sum | solution.py:125
  338.1 12.7 %fusion.8 = (f32[128]{0:T(128)S(1)}, f32[128]{0:T(128)S(1)}, f32[128,2048]{1,0:T(8,128)}) fusion(f32[128,2048]{1,0:T(8,128)} %param.10, s32[128]{0:T(128)S(1)} %iota_add_fusion, bf16[128,4096]{1,0:T(8,128)(2,1)S(1)} %copy-done.2, bf16[2048,4096]{1,0:T(8,128)(2,1)} %all-gather.5.cloned.1.call-done), kind=kOutput, calls=%fused_computation.32 | convolution fusion | flops 2149318656 | bytes 19924480 | tf_op jit(solution)/shard_map/rp,mp->rm/dot_general | solution.py:35
  350.8 23.4 %all-gather.2 = f32[16,1,128]{2,1,0:T(1,128)S(1)} all-gather(f32[1,1,128]{2,1,0:T(1,128)S(1)} %get-tuple-element.28), channel_id=1, replica_groups=mesh['group'=16,'dp'=16] {'dp'}, dimensions={0}, use_global_device_ids=true | all-gather | bytes 8704 | tf_op jit(solution)/shard_map/all_gather | solution.py:60
  374.2 23.4 %all-gather.1 = f32[16,1,128]{2,1,0:T(1,128)S(1)} all-gather(f32[1,1,128]{2,1,0:T(1,128)S(1)} %get-tuple-element.26), channel_id=1, replica_groups=mesh['group'=16,'dp'=16] {'dp'}, dimensions={0}, use_global_device_ids=true | all-gather | bytes 8704 | tf_op jit(solution)/shard_map/all_gather | solution.py:59
  397.6 12.2 %fusion.1 = f32[128,4096]{1,0:T(8,128)} fusion(f32[128,4096]{1,0:T(8,128)} %reduce_sum.148, bf16[2048,4096]{1,0:T(8,128)(2,1)} %all-gather.5.cloned.1.call-done, f32[128]{0:T(128)S(1)} %copy-done.7, f32[128,2048]{1,0:T(8,128)} %get-tuple-element.32, f32[128,2048]{1,0:T(8,128)} %param.10, f32[2048]{0:T(1024)S(1)} %bitcast.51, f32[2048]{0:T(1024)S(1)} %bitcast.52, ...), kind=kOutput, calls=%fused_computation.8 | convolution fusion | flops 2157182976 | bytes 24144384 | tf_op jit(solution)/shard_map/dot_general | solution.py:75
  409.9 3.5 multiply_reduce_fusion.1
  413.4 1.4 copy-done.5
  414.8 5.8 convert_bitcast_fusion
  420.7 0.2 fusion.27
  420.9 0.8 copy-done.3
  421.8 2.0 multiply_reduce_fusion.5
  423.8 0.6 multiply_reduce_fusion.6
  424.4 170.6 %psum.7 = f32[]{:T(128)} all-reduce(f32[]{:T(128)} %multiply_reduce_fusion.6), channel_id=1, replica_groups=mesh['group'=16,'dp'=16] {'group','dp'}, use_global_device_ids=true, to_apply=%region_15.16 | all-reduce | flops 1 | bytes 8 | tf_op jit(solution)/shard_map/psum | solution.py:139
  595.7 2.0 copy.27
  597.7 7.6 %convolution_convert_fusion.3 = bf16[128,1024]{1,0:T(8,128)(2,1)} fusion(bf16[1024,4096]{1,0:T(8,128)(2,1)} %param.11, f32[128,4096]{1,0:T(8,128)S(1)} %get-tuple-element.31, f32[128,4096]{1,0:T(8,128)} %copy-done.5, f32[128]{0:T(128)S(1)} %get-tuple-element.24, f32[128]{0:T(128)S(1)} %get-tuple-element.35, f32[128]{0:T(128)S(1)} %get-tuple-element.25), kind=kOutput, calls=%fused_computation.23 | convolution fusion | flops 1076494336 | bytes 12846592 | tf_op jit(solution)/shard_map/rp,dp->rd/dot_general | solution.py:146
  605.4 58.1 %reduce-scatter.7.cloned.1.call-done = bf16[64,256]{1,0:T(8,128)(2,1)} async-done(((bf16[1024,256]{1,0:T(8,128)(2,1)}), bf16[64,256]{1,0:T(8,128)(2,1)}) %reduce-scatter.7.cloned.1.call-update) | async-done | bytes 32784
  663.5 0.9 copy.28
  664.4 0.7 copy.26
  (46 shorter events, 1.1 us)
Async XLA Ops:
  7.2 1.0 copy-start
  7.2 5.7 copy-start.4
  7.2 330.9 %all-gather.5.cloned.1.call-start = ((), (), s32[]{:S(2)}) async-start(), calls=%async_computation.6 | async-start | bytes 17825792 | tf_op jit(solution)/shard_map/all_gather | solution.py:34
  13.2 2.2 copy-start.8
  13.2 3.4 copy-start.9
  36.5 5.0 copy-start.2
  36.5 202.7 %all-to-all-start.2 = ((bf16[16,24,4096]{2,1,0:T(8,128)(2,1)}), bf16[16,24,4096]{2,1,0:T(8,128)(2,1)}, u32[]{:S(2)}, u32[]{:S(2)}) async-start(bf16[16,24,4096]{2,1,0:T(8,128)(2,1)} %bitcast.49), calls=%async_computation.2 | async-start | bytes 6291456 | tf_op jit(solution)/shard_map/all_to_all | solution.py:105
  239.2 56.4 %all-to-all-start.1 = ((bf16[16,24,4096]{2,1,0:T(8,128)(2,1)}), bf16[16,24,4096]{2,1,0:T(8,128)(2,1)}, u32[]{:S(2)}, u32[]{:S(2)}) async-start(bf16[16,24,4096]{2,1,0:T(8,128)(2,1)} %bitcast.48), calls=%async_computation.1 | async-start | bytes 6291456 | tf_op jit(solution)/shard_map/all_to_all | solution.py:104
  260.0 6.1 copy-start.6
  260.0 6.1 copy-start.7
  295.6 6.6 copy-start.1
  305.1 104.7 %all-to-all-start.3 = ((bf16[16,24,4096]{2,1,0:T(8,128)(2,1)}), bf16[16,24,4096]{2,1,0:T(8,128)(2,1)}, u32[]{:S(2)}, u32[]{:S(2)}) async-start(bf16[16,24,4096]{2,1,0:T(8,128)(2,1)} %bitcast.47), calls=%async_computation.3 | async-start | bytes 6291456 | tf_op jit(solution)/shard_map/all_to_all | solution.py:132
  318.7 277.0 %reduce-scatter.5.cloned.1.call-start = ((), (), s32[]{:S(2)}) async-start(), calls=%async_computation.7 | async-start | bytes 8912896 | tf_op jit(solution)/shard_map/reduce_scatter | solution.py:152
  413.4 1.4 copy-start.5
  420.5 1.2 copy-start.3
  420.6 243.0 %reduce-scatter.7.cloned.1.call-start = ((), (), s32[]{:S(2)}) async-start(), calls=%async_computation.8 | async-start | bytes 557056
Sparse Core Ops, SparseCore 0:
  15.5 214.3 all-gather.4
  420.7 111.8 reduce-scatter.4
  597.9 65.6 reduce-scatter.6
where the time goes:
time: 675 us; the launch traced here: 673 us
  blocking collectives  257 us (38%)
  waiting for transfers between devices  253 us (37%)
  matrix products  66 us (10%)
  local copies, waits for them, and re-layouts  36.5 us (5%)
  starting transfers between devices  23.3 us (3%)
  other arithmetic  20.5 us (3%)
  between operations  15.7 us (2%)
    all_to_all x1, waiting for transfers between devices, local(): lax.all_to_all(sent_teacher, 'group', split_axis=0, concat_axis=0, tiled=...  195 us
    psum x1, blocking collectives, local(): loss_total = lax.psum(local_loss, ('group', 'dp'))  171 us
    unnamed x4, waiting for transfers between devices  58.2 us
    all_gather x1, blocking collectives, local(): lax.all_gather(text_weight, 'dp', axis=0, tiled=True)  24.8 us
    all_gather x1, blocking collectives, local(): lax.all_gather(log_s, 'dp', axis=0, tiled=True)  23.4 us
    all_gather x1, blocking collectives, local(): lax.all_gather(log_t, 'dp', axis=0, tiled=True)  23.4 us
    all_to_all x1, blocking collectives, local(): lax.all_to_all(request, 'group', split_axis=0, concat_axis=0, tiled=True)  15.2 us
    all_to_all x1, starting transfers between devices, local(): lax.all_to_all(slotted, 'group', split_axis=0, concat_axis=0, tiled=True)  13.6 us
  transfers between devices with their start and end apart: 6, of which 2 were waited for; matrix products, arithmetic and copies ran while one was open for 15% of the time, Pallas kernels for 0%

commit v1 on v0

v1 whole, which is shorter than its diff:
```python
import jax
import jax.numpy as jnp
from jax import lax
from jax.sharding import PartitionSpec as P

HARD = 2
EPSILON = 1e-06
SOFTMAX_TEMP = 0.05
SIMILARITY_COEF = 200.0
HARD_WEIGHT = 20.0
LOSS_SCALE = 1024.0


def row_norms(values):
    return jnp.sqrt(jnp.sum(values * values, 1, keepdims=True) + EPSILON)


def dot_t(left, right):
    return lax.dot_general(
        left, right, (((1,), (1,)), ((), ())), preferred_element_type=jnp.float32
    )


def two_part_dot_t(left, right):
    high = left.astype(jnp.bfloat16)
    low = (left - high.astype(jnp.float32)).astype(jnp.bfloat16)
    both = dot_t(jnp.concatenate([high, low], 0), right)
    rows = left.shape[0]
    return both[:rows] + both[rows:]


def local(
    student, teacher, teacher_similarity, projector, hard_group, hard_local, hard_count, text_weight
):
    rows = student.shape[0]
    groups = lax.axis_size("group")
    columns = lax.axis_size("dp")
    set_count = rows * columns
    position = lax.axis_index("dp")
    my_group = lax.axis_index("group")
    student_set = lax.all_gather(student, "dp", axis=0, tiled=True)
    student_col = lax.all_gather(student, "group", axis=0, tiled=True)
    teacher_float = teacher.astype(jnp.float32)
    teacher_unit = (teacher_float / row_norms(teacher_float)).astype(jnp.bfloat16)
    teacher_cols = lax.all_to_all(teacher_unit, "group", split_axis=1, concat_axis=0, tiled=True)
    projected = jnp.dot(student, projector, preferred_element_type=jnp.float32)
    norm = row_norms(projected)
    cosine = jnp.sum(projected * teacher_unit.astype(jnp.float32), 1, keepdims=True)
    back = dot_t(projected.astype(jnp.bfloat16), projector)
    target = (hard_group * rows + hard_local).astype(jnp.float32)
    order = jnp.arange(HARD, dtype=jnp.int32)[None, :]
    count = hard_count[:, None]
    entry_weight = (
        (order < count).astype(jnp.float32) * HARD_WEIGHT / count.astype(jnp.float32)
    ) * text_weight[:, None]
    own_index = position * rows + jnp.arange(rows, dtype=jnp.int32)
    off_diagonal = jnp.arange(set_count, dtype=jnp.int32)[None, :] != own_index[:, None]
    teacher_scaled = teacher_similarity / SOFTMAX_TEMP
    teacher_exp = jnp.where(off_diagonal, jnp.exp(teacher_scaled), 0.0)
    total_t = jnp.sum(teacher_exp, 1, keepdims=True)
    facts = jnp.concatenate(
        [norm, 1.0 / total_t, text_weight[:, None], target, entry_weight], 1
    ).T
    facts_set = lax.all_gather(facts[:3], "dp", axis=1, tiled=True)
    facts_col = lax.all_gather(facts, "group", axis=1, tiled=True)

    gram = dot_t(teacher_cols, teacher_cols)
    ids = jnp.arange(groups * rows, dtype=jnp.int32).astype(jnp.float32)
    part = jnp.stack(
        [jnp.sum(jnp.where(ids[:, None] == facts_col[3 + k][None, :], gram, 0.0), 0) for k in range(HARD)]
    )
    teacher_hard = lax.psum(part, "group")

    norm_set, total_t_set, weight_set = facts_set[0][None], facts_set[1][None], facts_set[2][None]
    similarity = two_part_dot_t(back / norm, student_set) / norm_set
    student_exp = jnp.where(off_diagonal, jnp.exp(similarity / SOFTMAX_TEMP), 0.0)
    total_s = jnp.sum(student_exp, 1, keepdims=True)
    total_s_set = lax.all_gather((1.0 / total_s)[:, 0], "dp", axis=0, tiled=True)[None]
    gap = similarity - teacher_similarity
    weight = text_weight[:, None]
    sim_term = SIMILARITY_COEF / set_count * jnp.sum(gap * gap, 1, keepdims=True)
    kl_term = (
        jnp.sum(teacher_exp * gap, 1, keepdims=True) * (-1.0 / SOFTMAX_TEMP) / total_t
        + jnp.log(total_s)
        - jnp.log(total_t)
    )
    pair = (2.0 * SIMILARITY_COEF / set_count) * gap * (weight + weight_set) + (
        student_exp * (weight / total_s + weight_set * total_s_set)
        - teacher_exp * (weight / total_t + weight_set * total_t_set)
    ) / SOFTMAX_TEMP
    set_part = jnp.dot(
        (pair / norm_set).astype(jnp.bfloat16), student_set, preferred_element_type=jnp.float32
    )

    norm_col = facts_col[0][None]
    cross = two_part_dot_t(back / norm, student_col) / norm_col
    own_hard = lax.dynamic_slice_in_dim(teacher_hard, my_group * rows, rows, 1)
    own_ids = (my_group * rows + jnp.arange(rows, dtype=jnp.int32)).astype(jnp.float32)[:, None]
    hard = jnp.zeros_like(cross)
    hard_loss = 0.0
    for k in range(HARD):
        asked = jnp.where(ids[None, :] == target[:, k : k + 1], entry_weight[:, k : k + 1], 0.0)
        difference = cross - own_hard[k][:, None]
        hard = hard + asked * difference
        hard_loss = hard_loss + jnp.sum(asked * difference * difference)
        listed = jnp.where(facts_col[3 + k][None] == own_ids, facts_col[5 + k][None], 0.0)
        hard = hard + listed * (cross - teacher_hard[k][None])
    hard_part = jnp.dot(
        (2.0 * hard / norm_col).astype(jnp.bfloat16),
        student_col,
        preferred_element_type=jnp.float32,
    )
    local_loss = jnp.sum(weight * (1.0 - cosine / norm + sim_term + kl_term)) + hard_loss
    mean_loss = lax.psum(local_loss, ("group", "dp")) / (rows * groups * columns)

    combined = LOSS_SCALE * (set_part + hard_part)
    inner = jnp.sum(back * combined, 1, keepdims=True) - LOSS_SCALE * weight * cosine
    inside = combined / norm - student.astype(jnp.float32) * (inner / (norm * norm * norm))
    high = inside.astype(jnp.bfloat16)
    low = (inside - high.astype(jnp.float32)).astype(jnp.bfloat16)
    both = jnp.dot(
        jnp.concatenate([high, low], 0), projector, preferred_element_type=jnp.float32
    )
    proj_gradient = (
        both[:rows]
        + both[rows:]
        - (LOSS_SCALE * weight / norm) * teacher_unit.astype(jnp.float32)
    ).astype(jnp.bfloat16)
    student_gradient = dot_t(proj_gradient, projector).astype(jnp.bfloat16)
    gradient_cols = lax.all_to_all(proj_gradient, "dp", split_axis=1, concat_axis=0, tiled=True)
    within = lax.dot_general(
        student_set, gradient_cols, (((0,), (0,)), ((), ())), preferred_element_type=jnp.float32
    ).astype(jnp.bfloat16)
    projector_gradient = lax.psum_scatter(within, "group", scatter_dimension=0, tiled=True).astype(
        jnp.float32
    )
    return (mean_loss, student_gradient, projector_gradient)


def solution(mesh):
    return jax.shard_map(
        local,
        mesh=mesh,
        in_specs=(
            P(("group", "dp"), None),
            P(("group", "dp"), None),
            P(("group", "dp"), None),
            P(),
            P(("group", "dp"), None),
            P(("group", "dp"), None),
            P(("group", "dp")),
            P(("group", "dp")),
        ),
        out_specs=(P(), P(("group", "dp"), None), P("group", "dp")),
        check_vma=False,
    )
```

time: 675 us -> 331 us (0.49)
  waiting for transfers between devices: 253 us -> 1.44 us
  local copies, waits for them, and re-layouts: 36.5 us -> 5.29 us
  matrix products: 66 us -> 38.7 us
  other arithmetic: 20.5 us -> 5.34 us
  starting transfers between devices: 23.3 us -> 8.55 us
    all_to_all x3 -> x1, waiting for transfers between devices: 195 us -> 0.01 us  [local(): lax.all_to_all(teacher_unit, 'group', split_axis=1, concat_axis=0, tiled=...]
    unnamed x4, waiting for transfers between devices: 58.2 us -> 1.39 us
    dot_general x10 -> x9, matrix products: 61.3 us -> 32.3 us  [the longest x5 25.8 us: dot_t(): lax.dot_general(left, right, (((1,), (1,)), ((), ())), preferred_element_...]
    psum x1 -> x2, blocking collectives: 171 us -> 147 us  [the longest x1 87 us: local(): lax.psum(local_loss, ('group', 'dp')) / (rows * groups * columns)]
    all_gather x3, blocking collectives: 71.5 us -> 88.1 us  [the longest x1 34.3 us: local(): facts_set = lax.all_gather(facts[:3], 'dp', axis=1, tiled=True)]
    all_to_all x3 -> x1, starting transfers between devices: 23.2 us -> 8.44 us  [local(): lax.all_to_all(teacher_unit, 'group', split_axis=1, concat_axis=0, tiled=...]
    convert_element_type x2 -> x0, local copies, waits for them, and re-layouts: 12.1 us -> none  [the longest x1 6.06 us: local(): query_teacher = jnp.repeat(teacher_unit, HARD, axis=0).astype(jnp.float32)]
    reduce_sum x7 -> x3, other arithmetic: 14.1 us -> 2.43 us  [the longest x1 1.32 us: local(): hard_loss = hard_loss + jnp.sum(asked * difference * difference)]
  transfers between devices with their start and end apart: 6 -> 4, of which waited for: 2 -> 0; matrix products, arithmetic and copies ran while one was open for 15% -> 10% of each run, Pallas kernels for 0% -> 0%
where the time goes in v1:
time: 331 us; the launch traced here: 330 us
  blocking collectives  253 us (76%)
  matrix products  38.7 us (12%)
  between operations  17.7 us (5%)
  starting transfers between devices  8.55 us (3%)
  other arithmetic  5.34 us (2%)
  local copies, waits for them, and re-layouts  5.29 us (2%)
    psum x1, blocking collectives, local(): lax.psum(local_loss, ('group', 'dp')) / (rows * groups * columns)  87 us
    psum x1, blocking collectives, local(): teacher_hard = lax.psum(part, 'group')  59.8 us
    all_gather x1, blocking collectives, local(): facts_set = lax.all_gather(facts[:3], 'dp', axis=1, tiled=True)  34.3 us
    all_gather x1, blocking collectives, local(): facts_col = lax.all_gather(facts, 'group', axis=1, tiled=True)  30.2 us
    dot_general x5, matrix products, dot_t(): lax.dot_general(left, right, (((1,), (1,)), ((), ())), preferred_element_...  25.8 us
    all_gather x1, blocking collectives, local(): lax.all_gather((1.0 / total_s)[:, 0], 'dp', axis=0, tiled=True)[None]  23.6 us
    all_to_all x1, blocking collectives, local(): lax.all_to_all(proj_gradient, 'dp', split_axis=1, concat_axis=0, tiled=True)  18.5 us
    all_to_all x1, starting transfers between devices, local(): lax.all_to_all(teacher_unit, 'group', split_axis=1, concat_axis=0, tiled=...  8.44 us
  transfers between devices with their start and end apart: 4, of which 0 were waited for; matrix products, arithmetic and copies ran while one was open for 10% of the time, Pallas kernels for 0%

profile of v1, /device:TPU:1, one launch (start us, length us, event | category | flops | bytes accessed | tf_op | source)
XLA Modules:
  0.0 330.4 jit_solution(17231246980006837051)
XLA Ops:
  7.2 0.0 all-gather.4.cloned.1.call-start
  7.2 0.7 all-gather.4.cloned.1.call-update
  7.9 0.0 all-gather.6.cloned.1.call-start
  7.9 0.7 all-gather.6.cloned.1.call-update
  8.6 1.5 fusion
  10.2 6.4 %fusion.2 = (f32[128]{0:T(128)S(1)}, f32[128]{0:T(128)S(1)}, bf16[128,4096]{1,0:T(8,128)(2,1)S(1)}, bf16[128,4096]{1,0:T(8,128)(2,1)}) fusion(f32[128]{0:T(128)S(1)} %add_sqrt_fusion.1, bf16[128,4096]{1,0:T(8,128)(2,1)} %param.9, bf16[128,1024]{1,0:T(8,128)(2,1)} %param.8, bf16[1024,4096]{1,0:T(8,128)(2,1)} %param.11), kind=kOutput, calls=%fused_computation.8 | convolution fusion | flops 1078460160 | bytes 11798016 | tf_op jit(solution)/shard_map/dot_general | solution.py:46
  16.6 0.0 copy-start.3
  16.6 0.0 copy-start.4
  16.6 1.1 copy.25
  17.7 8.4 %all-to-all-start = ((bf16[128,16,256]{2,0,1:T(8,128)(2,1)}), bf16[128,16,256]{2,0,1:T(8,128)(2,1)S(1)}, u32[]{:S(2)}, u32[]{:S(2)}) async-start(bf16[128,16,256]{2,0,1:T(8,128)(2,1)} %bitcast.66), calls=%async_computation | async-start | bytes 2097152 | tf_op jit(solution)/shard_map/all_to_all | solution.py:45
  26.1 0.0 reduce-scatter.4.cloned.1.call-start
  26.1 0.0 copy-done.5
  26.2 0.0 copy-done
  26.2 0.3 fusion.12
  26.6 0.0 copy-done.2
  26.6 0.0 copy-done.3
  26.6 34.3 %all_gather.16 = f32[3,2048]{1,0:T(4,128)S(1)} all-gather(f32[3,128]{1,0:T(4,128)S(1)} %slice.73), channel_id=1, replica_groups=mesh['group'=16,'dp'=16] {'dp'}, dimensions={1}, use_global_device_ids=true | all-gather | bytes 26112 | tf_op jit(solution)/shard_map/all_gather | solution.py:64
  60.9 30.2 %all_gather.18 = f32[7,2048]{1,0:T(8,128)S(1)} all-gather(f32[7,128]{1,0:T(8,128)S(1)} %bitcast.79), channel_id=1, replica_groups=mesh['group'=16,'dp'=16] {'group'}, dimensions={1}, use_global_device_ids=true | all-gather | bytes 60928 | tf_op jit(solution)/shard_map/all_gather | solution.py:65
  91.2 7.6 %fusion.37 = (bf16[128,1024]{1,0:T(8,128)(2,1)}, bf16[128,1024]{1,0:T(8,128)(2,1)}, f32[128,1024]{1,0:T(8,128)}) fusion(f32[128]{0:T(128)S(1)} %get-tuple-element.50, bf16[1024,4096]{1,0:T(8,128)(2,1)} %param.11, bf16[128,4096]{1,0:T(8,128)(2,1)} %get-tuple-element.52), kind=kOutput, calls=%fused_computation.69 | convolution fusion | flops 1074397184 | bytes 10486272 | tf_op jit(solution)/shard_map/dot_general | solution.py:19
  98.8 0.0 all-to-all-done
  98.8 3.8 %select_reduce_fusion.1 = (f32[2048]{0:T(1024)S(1)}, f32[2048]{0:T(1024)S(1)}) fusion(f32[2048]{0:T(1024)S(1)} %bitcast.84, f32[2048]{0:T(1024)S(1)} %iota_convert_fusion, f32[2048]{0:T(1024)S(1)} %bitcast.82, bf16[2048,256]{1,0:T(8,128)(2,1)S(1)} %bitcast.72), kind=kOutput, calls=%fused_computation.1 | convolution fusion | flops 2172645376 | bytes 1089536 | tf_op jit(solution)/shard_map/dot_general | solution.py:19
  102.6 59.8 %psum.14 = f32[2,2048]{1,0:T(2,128)S(1)} all-reduce(f32[2,2048]{1,0:T(2,128)S(1)} %pad_maximum_fusion.3), channel_id=1, replica_groups=mesh['group'=16,'dp'=16] {'group'}, use_global_device_ids=true, to_apply=%region_10.11 | all-reduce | flops 4096 | bytes 32768 | tf_op jit(solution)/shard_map/psum | solution.py:72
  162.5 0.0 all-gather.4.cloned.1.call-done
  162.5 3.6 %fusion.36 = f32[256,2048]{1,0:T(8,128)S(1)} fusion(bf16[2048,1024]{1,0:T(8,128)(2,1)} %all-gather.4.cloned.1.call-done, bf16[128,1024]{1,0:T(8,128)(2,1)} %get-tuple-element.27, bf16[128,1024]{1,0:T(8,128)(2,1)} %get-tuple-element.26), kind=kOutput, calls=%fused_computation.67 | convolution fusion | flops 1074790400 | bytes 6815744 | tf_op jit(solution)/shard_map/dot_general | solution.py:19
  166.1 0.8 multiply_reduce_fusion.4
  166.9 23.6 %all-gather = f32[16,1,128]{2,1,0:T(1,128)S(1)} all-gather(f32[1,1,128]{2,1,0:T(1,128)S(1)} %get-tuple-element.48), channel_id=1, replica_groups=mesh['group'=16,'dp'=16] {'dp'}, dimensions={0}, use_global_device_ids=true | all-gather | bytes 8704 | tf_op jit(solution)/shard_map/all_gather | solution.py:78
  190.6 0.0 all-gather.6.cloned.1.call-done
  190.6 0.0 copy-start.6
  190.6 3.8 %fusion.35 = f32[256,2048]{1,0:T(8,128)S(1)} fusion(bf16[2048,1024]{1,0:T(8,128)(2,1)} %all-gather.6.cloned.1.call-done, bf16[128,1024]{1,0:T(8,128)(2,1)} %get-tuple-element.27, bf16[128,1024]{1,0:T(8,128)(2,1)} %get-tuple-element.26), kind=kOutput, calls=%fused_computation.66 | convolution fusion | flops 1074790400 | bytes 6815744 | tf_op jit(solution)/shard_map/dot_general | solution.py:19
  194.4 1.3 multiply_reduce_fusion.1
  195.7 1.4 fusion.34
  197.1 0.8 copy-done.7
  197.9 0.1 copy-done.8
  198.0 1.5 multiply_reduce_fusion.5
  199.5 0.6 fusion.40
  200.1 0.2 fusion.51
  200.3 0.5 slice-done.1
  200.8 2.3 fusion.13
  203.1 0.5 fusion.4
  203.6 0.1 copy.24
  203.7 18.5 %all_to_all.38 = bf16[128,16,256]{2,0,1:T(8,128)(2,1)S(1)} all-to-all(bf16[128,16,256]{2,0,1:T(8,128)(2,1)S(1)} %bitcast.71), channel_id=1, replica_groups=mesh['group'=16,'dp'=16] {'dp'}, dimensions={1} | all-to-all | bytes 2097152 | tf_op jit(solution)/shard_map/all_to_all | solution.py:130
  222.2 1.3 fusion.5
  223.5 1.0 copy.18
  224.5 0.0 reduce-scatter.4.cloned.1.call-update
  226.5 87.0 %psum.15 = f32[]{:T(128)} all-reduce(f32[]{:T(128)S(6)} %add.152), channel_id=1, replica_groups=mesh['group'=16,'dp'=16] {'group','dp'}, use_global_device_ids=true, to_apply=%region_13.14 | all-reduce | flops 1 | bytes 8 | tf_op jit(solution)/shard_map/psum | solution.py:114
  314.1 7.0 %convolution_convert_fusion.1 = bf16[128,1024]{1,0:T(8,128)(2,1)} fusion(bf16[128,4096]{1,0:T(8,128)(2,1)S(1)} %fusion.4, bf16[1024,4096]{1,0:T(8,128)(2,1)} %param.11), kind=kOutput, calls=%fused_computation.17 | convolution fusion | flops 1073872896 | bytes 9699328 | tf_op jit(solution)/shard_map/dot_general | solution.py:19
  321.1 0.9 copy.19
  322.0 0.7 copy.17
  (35 shorter events, 0.2 us)
Async XLA Ops:
  7.2 155.3 %all-gather.4.cloned.1.call-start = ((), (), s32[]{:S(2)}) async-start(), calls=%async_computation.3 | async-start | bytes 4456448 | tf_op jit(solution)/shard_map/all_gather | solution.py:41
  7.9 182.7 %all-gather.6.cloned.1.call-start = ((), (), s32[]{:S(2)}) async-start(), calls=%async_computation.4 | async-start | bytes 4456448 | tf_op jit(solution)/shard_map/all_gather | solution.py:42
  16.5 9.6 %copy-start.5 = (s32[128]{0:T(128)S(1)}, s32[128]{0:T(128)}, u32[]{:S(2)}) copy-start(s32[128]{0:T(128)} %param.14) | copy-start | bytes 1540
  16.5 9.6 %copy-start = (f32[128,2048]{1,0:T(8,128)S(1)}, f32[128,2048]{1,0:T(8,128)}, u32[]{:S(2)}) copy-start(f32[128,2048]{1,0:T(8,128)} %param.10) | copy-start | bytes 3145732
  16.6 10.0 %copy-start.2 = (f32[128]{0:T(128)S(1)}, f32[128]{0:T(128)}, u32[]{:S(2)}) copy-start(f32[128]{0:T(128)} %param.15) | copy-start | bytes 1540
  16.6 10.0 %copy-start.3 = (s32[128,2]{0,1:T(2,128)S(1)}, s32[128,2]{0,1:T(2,128)}, u32[]{:S(2)}) copy-start(s32[128,2]{0,1:T(2,128)} %param.13) | copy-start | bytes 3076
  16.6 10.0 %copy-start.4 = (s32[128,2]{0,1:T(2,128)S(1)}, s32[128,2]{0,1:T(2,128)}, u32[]{:S(2)}) copy-start(s32[128,2]{0,1:T(2,128)} %param.12) | copy-start | bytes 3076
  17.7 81.1 %all-to-all-start = ((bf16[128,16,256]{2,0,1:T(8,128)(2,1)}), bf16[128,16,256]{2,0,1:T(8,128)(2,1)S(1)}, u32[]{:S(2)}, u32[]{:S(2)}) async-start(bf16[128,16,256]{2,0,1:T(8,128)(2,1)} %bitcast.66), calls=%async_computation | async-start | bytes 2097152 | tf_op jit(solution)/shard_map/all_to_all | solution.py:45
  26.1 295.0 %reduce-scatter.4.cloned.1.call-start = ((), (), s32[]{:S(2)}) async-start(), calls=%async_computation.5 | async-start | bytes 557056
  190.6 5.1 %copy-start.6 = (bf16[2048,1024]{1,0:T(8,128)(2,1)S(1)}, bf16[2048,1024]{1,0:T(8,128)(2,1)}, u32[]{:S(2)}) copy-start(bf16[2048,1024]{1,0:T(8,128)(2,1)} %all-gather.4.cloned.1.call-done) | copy-start | bytes 12582916
  195.7 2.2 copy-start.7
  195.7 2.3 copy-start.8
  195.7 4.6 %slice-start = ((s8[8388608]{0:T(1024)(128)(4,1)}), s8[4194304]{0:T(1024)(128)(4,1)S(1)}, s32[]{:S(2)}) async-start(s8[8388608]{0:T(1024)(128)(4,1)} %bitcast.68), calls=%async_computation.6 | async-start | bytes 8388608
  198.0 2.1 copy-start.1
  198.0 2.8 slice-start.1
Sparse Core Ops, SparseCore 0:
  9.8 78.4 all-gather.3
  90.9 68.3 all-gather.5
  224.7 80.8 reduce-scatter.3

commit v2 on v1

v2 whole, which is shorter than its diff:
```python
import functools
import jax
import jax.numpy as jnp
from jax import lax
from jax.experimental import pallas as pl
from jax.experimental.pallas import tpu as pltpu
from jax.sharding import PartitionSpec as P

HARD = 2
EPSILON = 1e-06
INVERSE_TEMP = 20.0
SIMILARITY_COEF = 200.0
HARD_WEIGHT = 20.0
LOSS_SCALE = 1024.0
MESH = pl.DeviceIdType.MESH
F32 = jnp.float32
BF16 = jnp.bfloat16


def dot(left, right):
    return jnp.dot(left, right, preferred_element_type=F32)


def dot_t(left, right):
    return lax.dot_general(left, right, (((1,), (1,)), ((), ())), preferred_element_type=F32)


def loop(low, high, body):
    def step(i, carry):
        body(i)
        return carry

    lax.fori_loop(low, high, step, 0)


def kernel(
    groups,
    columns,
    student,
    teacher,
    sims,
    projector,
    hard_group,
    hard_local,
    hard_count,
    text_weight,
    loss_out,
    student_out,
    projector_out,
    s_set,
    s_col,
    s_turned,
    proj,
    teach,
    sim_t,
    unit_t,
    cols_t,
    sim_s,
    exp_s,
    exp_t,
    row_total,
    h_mat,
    w_mat,
    back,
    comb,
    pair_rows,
    grad,
    grad_cols,
    facts,
    facts_set,
    facts_col,
    part,
    parts,
    hard_sum,
    totals,
    totals_set,
    within,
    arrived,
    loss_tile,
    loss_set,
    loss_tile2,
    loss_col,
    local_sem,
    set_send,
    set_recv,
    col_send,
    col_recv,
    unit_send,
    unit_recv,
    fset_send,
    fset_recv,
    fcol_send,
    fcol_recv,
    part_send,
    part_recv,
    tot_send,
    tot_recv,
    grad_send,
    grad_recv,
    out_send,
    out_recv,
    lset_send,
    lset_recv,
    lcol_send,
    lcol_recv,
):
    rows, width = student.shape
    chunk = unit_t.shape[2]
    count = unit_t.shape[0]
    half = rows // 2
    set_count = rows * columns
    g = lax.axis_index("group")
    d = lax.axis_index("dp")
    xs, zs = groups // 4, columns // 2
    x, yh, core = g // 4, lax.rem(g // 2, 2), lax.rem(g, 2)
    yl, z = d // zs, lax.rem(d, zs)

    def flip(value, by):
        return 1 - value if by else value

    def col_id(dx, fy, fc):
        return lax.rem(x + dx % xs, xs) * 4 + flip(yh, fy) * 2 + flip(core, fc)

    def set_id(fy, dz):
        return flip(yl, fy) * zs + lax.rem(z + dz % zs, zs)

    def rows_of(block):
        return pl.ds(pl.multiple_of(block * rows, rows), rows)

    def lanes_of(block):
        return pl.ds(pl.multiple_of(block * rows, rows), rows)

    def chunk_of(q):
        return pl.ds(pl.multiple_of(q * chunk, chunk), chunk)

    def copy(src, dst, send, recv, group, column):
        return pltpu.make_async_remote_copy(
            src_ref=src,
            dst_ref=dst,
            send_sem=send,
            recv_sem=recv,
            device_id=(group, column),
            device_id_type=MESH,
        )

    local = [
        pltpu.make_async_copy(student, s_set.at[rows_of(d)], local_sem.at[0]),
        pltpu.make_async_copy(student, s_col.at[rows_of(g)], local_sem.at[1]),
        pltpu.make_async_copy(teacher, teach, local_sem.at[2]),
        pltpu.make_async_copy(projector, proj, local_sem.at[3]),
        pltpu.make_async_copy(sims, sim_t, local_sem.at[4]),
    ]
    for one in (2, 0, 1, 3, 4):
        local[one].start()

    barrier = pltpu.get_barrier_semaphore()

    def greet(o):
        pl.semaphore_signal(
            barrier, inc=1, device_id=(g, lax.rem(d + o, columns)), device_id_type=MESH
        )
        pl.semaphore_signal(
            barrier, inc=1, device_id=(lax.rem(g + o, groups), d), device_id_type=MESH
        )

    loop(1, columns, greet)
    pl.semaphore_wait(barrier, 2 * (columns - 1))

    pending = []

    def region(ref, block, part_of):
        start = pl.multiple_of(block * rows, rows)
        if part_of is None:
            return ref.at[pl.ds(start, rows)]
        return ref.at[pl.ds(pl.multiple_of(start + part_of * half, half), half)]

    def set_slot(fy, dz, part_of):
        return (fy * zs + dz % zs) * 2 + (part_of or 0)

    def send_set(fy, dz, to_fy, to_dz, part_of=None):
        block = set_id(fy, dz)
        place = region(s_set, block, part_of)
        source = student if (fy == 0 and dz == 0) else place
        one = copy(
            source,
            place,
            set_send.at[len([p for p in pending if p[0] == "set"])],
            set_recv.at[set_slot(fy ^ to_fy, dz - to_dz, part_of)],
            g,
            set_id(to_fy, to_dz),
        )
        one.start()
        pending.append(("set", one))

    def wait_set(fy, dz, part_of=None):
        place = region(s_set, set_id(fy, dz), part_of)
        slot = set_slot(fy, dz, part_of)
        copy(place, place, set_send.at[0], set_recv.at[slot], g, set_id(1, 0)).wait_recv()

    def col_slot(dx, fy, fc, part_of):
        return ((fy * 2 + fc) * xs + dx % xs) * 2 + (part_of or 0)

    def send_col(dx, fy, to_dx, to_fy, to_fc, part_of=None):
        block = col_id(dx, fy, 0)
        place = region(s_col, block, part_of)
        source = student if (fy == 0 and dx == 0) else place
        one = copy(
            source,
            place,
            col_send.at[len([p for p in pending if p[0] == "col"])],
            col_recv.at[col_slot(dx - to_dx, fy ^ to_fy, to_fc, part_of)],
            col_id(to_dx, to_fy, to_fc),
            d,
        )
        one.start()
        pending.append(("col", one))

    def wait_col(dx, fy, fc, part_of=None):
        place = region(s_col, col_id(dx, fy, fc), part_of)
        slot = col_slot(dx, fy, fc, part_of)
        copy(place, place, col_send.at[0], col_recv.at[slot], col_id(0, 0, 1), d).wait_recv()

    send_set(0, 0, 1, 0)
    send_set(0, 0, 0, 1)
    send_set(0, 0, 0, -1)
    send_col(0, 0, 0, 1, 0)
    send_col(0, 0, 1, 0, 0)
    send_col(0, 0, -1, 0, 0)
    send_col(0, 0, 0, 0, 1)

    def pass_set(step):
        if step == 0:
            wait_set(1, 0)
            send_set(1, 0, 0, 1)
            send_set(1, 0, 0, -1)
            return
        last = step == zs // 2 - 1
        for fy in (0, 1):
            wait_set(fy, -step)
            send_set(fy, -step, 0, 1, 0 if last else None)
            wait_set(fy, step)
            send_set(fy, step, 0, -1, 1 if last else None)

    def pass_col(step):
        if step == 0:
            wait_col(0, 1, 0)
            send_col(0, 1, 1, 0, 0)
            send_col(0, 1, -1, 0, 0)
            send_col(0, 1, 0, 0, 1)
        elif step == 1:
            for fy in (0, 1):
                wait_col(-1, fy, 0)
                send_col(-1, fy, 1, 0, 0, 0)
                send_col(-1, fy, 0, 0, 1)
                wait_col(1, fy, 0)
                send_col(1, fy, -1, 0, 0, 1)
                send_col(1, fy, 0, 0, 1)
        else:
            for fy in (0, 1):
                wait_col(2, fy, 0, 0)
                wait_col(2, fy, 0, 1)
                send_col(2, fy, 0, 0, 1)

    def exchange(src_of, dst, send, recv, along):
        me, size = (d, columns) if along == "dp" else (g, groups)

        def at(o):
            peer = lax.rem(me + o, size)
            where = (g, peer) if along == "dp" else (peer, d)
            return copy(src_of(peer), dst(me), send.at[o], recv.at[o], *where)

        def arrive(o):
            source = lax.rem(me + size - o, size)
            where = (g, source) if along == "dp" else (source, d)
            copy(dst(source), dst(source), send.at[o], recv.at[o], *where).wait_recv()

        return (
            lambda: loop(1, size, lambda o: at(o).start()),
            lambda: loop(1, size, arrive),
            lambda: loop(1, size, lambda o: at(o).wait_send()),
        )

    local[2].wait()

    def square_sum(q, total):
        t = teach[:, chunk_of(q)].astype(F32)
        t = t * t
        return total + sum(t[:, i : i + 128] for i in range(0, chunk, 128))

    t_total = lax.fori_loop(0, count, square_sum, jnp.zeros((rows, 128), F32))
    t_scale = 1.0 / jnp.sqrt(jnp.sum(t_total, 1, keepdims=True) + EPSILON)

    def make_unit(q):
        unit_t[q] = (teach[:, chunk_of(q)].astype(F32) * t_scale).astype(BF16)

    loop(0, count, make_unit)
    unit_start, unit_wait, unit_end = exchange(
        lambda peer: unit_t.at[peer], lambda me: cols_t.at[rows_of(me)], unit_send, unit_recv, "group"
    )
    unit_start()
    cols_t[rows_of(g)] = unit_t[g]

    local[0].wait()
    local[1].wait()
    local[3].wait()
    back[...] = jnp.zeros_like(back)

    def project(q, carry):
        squares, along = carry
        p = dot(s_set[rows_of(d)], proj[:, chunk_of(q)])
        both = p * unit_t[q].astype(F32)
        back[...] += dot_t(p.astype(BF16), proj[:, chunk_of(q)])
        for i in range(0, chunk, 128):
            piece = p[:, i : i + 128]
            squares = squares + piece * piece
            along = along + both[:, i : i + 128]
        return squares, along

    zero = jnp.zeros((rows, 128), F32)
    squares, along = lax.fori_loop(0, count, project, (zero, zero))
    norm = jnp.sqrt(jnp.sum(squares, 1, keepdims=True) + EPSILON)
    cosine = jnp.sum(along, 1, keepdims=True)
    inverse = 1.0 / norm

    def split_store(value):
        high = value.astype(BF16)
        pair_rows[0:rows] = high
        pair_rows[rows : 2 * rows] = (value - high.astype(F32)).astype(BF16)

    split_store(back[...] * inverse)
    pass_set(0)
    pass_col(0)

    sub = lax.broadcasted_iota(jnp.int32, (rows, rows), 0)
    lane = lax.broadcasted_iota(jnp.int32, (rows, rows), 1)
    eye = sub == lane

    def to_row(column):
        return jnp.sum(jnp.where(eye, column, 0.0), 0, keepdims=True)

    def to_column(row):
        return jnp.sum(jnp.where(eye, row, 0.0), 1, keepdims=True)

    local[4].wait()

    def teacher_exp(b, total):
        value = jnp.exp(sim_t[:, lanes_of(b)] * INVERSE_TEMP)
        value = jnp.where(jnp.logical_and(eye, b == d), 0.0, value)
        exp_t[b] = value
        return total + value

    total_t = jnp.sum(lax.fori_loop(0, columns, teacher_exp, zero), 1, keepdims=True)
    weight_row = text_weight[...]
    used = hard_count[...]
    facts[0:1, :] = to_row(inverse)
    facts[1:2, :] = to_row(1.0 / total_t)
    facts[2:3, :] = weight_row
    for k in range(HARD):
        facts[3 + k : 4 + k, :] = (
            hard_group[k : k + 1, :] * rows + hard_local[k : k + 1, :]
        ).astype(F32)
        facts[5 + k : 6 + k, :] = (
            jnp.where(used > k, HARD_WEIGHT / used.astype(F32), 0.0) * weight_row
        )
    facts[7:8, :] = jnp.zeros((1, rows), F32)
    facts_set[d] = facts[...]
    facts_col[g] = facts[...]
    fcol_start, fcol_wait, fcol_end = exchange(
        lambda peer: facts, lambda me: facts_col.at[me], fcol_send, fcol_recv, "group"
    )
    fset_start, fset_wait, fset_end = exchange(
        lambda peer: facts, lambda me: facts_set.at[me], fset_send, fset_recv, "dp"
    )
    fcol_start()
    fset_start()
    pass_set(1)
    pass_col(1)

    row_total[...] = zero

    def similarity(block):
        both = dot_t(pair_rows[...], s_set[rows_of(block)])
        value = (both[0:rows] + both[rows : 2 * rows]) * facts_set[block, 0:1, :]
        grown = jnp.exp(value * INVERSE_TEMP)
        grown = jnp.where(jnp.logical_and(eye, block == d), 0.0, grown)
        sim_s[block] = value
        exp_s[block] = grown
        row_total[...] += grown

    def turn(block):
        s_turned[:, lanes_of(block)] = s_set[rows_of(block)].T

    unit_wait()
    fcol_wait()
    step_rows = 512 if groups * rows >= 512 else groups * rows
    numbers = lax.broadcasted_iota(jnp.int32, (step_rows, rows), 0).astype(F32)

    def pick(b):
        queries = cols_t[rows_of(b)]
        sums = [jnp.zeros((1, rows), F32)] * HARD
        for c in range(0, groups * rows, step_rows):
            gram = dot_t(cols_t[c : c + step_rows], queries)
            for k in range(HARD):
                wanted = facts_col[b, 3 + k : 4 + k, :] - float(c)
                sums[k] = sums[k] + jnp.sum(
                    jnp.where(numbers == wanted, gram, 0.0), 0, keepdims=True
                )
        for k in range(HARD):
            part[pl.ds(k * groups + b, 1), :] = sums[k]

    loop(0, groups, pick)
    part_start, part_wait, part_end = exchange(
        lambda peer: part, lambda me: parts.at[me], part_send, part_recv, "group"
    )
    part_start()
    parts[g] = part[...]
    pass_set(2)
    pass_col(2)

    fset_wait()
    for fy, dz in ((0, 0), (1, 0), (0, -1), (0, 1), (1, -1), (1, 1)):
        similarity(set_id(fy, dz))
    pass_set(3)
    for fy, dz in ((0, -2), (0, 2), (1, -2), (1, 2)):
        similarity(set_id(fy, dz))

    for dx in range(xs):
        for fy in (0, 1):
            wait_col(dx, fy, 1)
    part_wait()
    hard_sum[...] = jnp.sum(parts[...], 0)
    weight = to_column(weight_row)
    own_hard = [to_column(hard_sum[pl.ds(k * groups + g, 1), :]) for k in range(HARD)]
    own_target = [to_column(facts[3 + k : 4 + k, :]) for k in range(HARD)]
    own_entry = [to_column(facts[5 + k : 6 + k, :]) for k in range(HARD)]
    own_ids = sub.astype(F32) + (g * rows).astype(F32)
    lane_ids = lane.astype(F32)

    def hard(b, loss):
        both = dot_t(pair_rows[...], s_col[rows_of(b)])
        scale = facts_col[b, 0:1, :]
        cross = (both[0:rows] + both[rows : 2 * rows]) * scale
        ids = lane_ids + (b * rows).astype(F32)
        value = jnp.zeros_like(cross)
        for k in range(HARD):
            asked = jnp.where(ids == own_target[k], own_entry[k], 0.0)
            difference = cross - own_hard[k]
            term = asked * difference
            loss = loss + term * difference
            listed = jnp.where(
                facts_col[b, 3 + k : 4 + k, :] == own_ids, facts_col[b, 5 + k : 6 + k, :], 0.0
            )
            value = value + term + listed * (cross - hard_sum[pl.ds(k * groups + b, 1), :])
        h_mat[:, lanes_of(b)] = (2.0 * scale * value).astype(BF16)
        return loss

    hard_loss = lax.fori_loop(0, groups, hard, zero)
    for fy, dz in ((0, -3), (0, 3), (1, -3), (1, 3)):
        similarity(set_id(fy, dz))
    for fy in (0, 1):
        wait_set(fy, zs // 2, 0)
        wait_set(fy, zs // 2, 1)
        similarity(set_id(fy, zs // 2))

    total_s = jnp.sum(row_total[...], 1, keepdims=True)
    totals[...] = jnp.broadcast_to(to_row(1.0 / total_s), totals.shape)
    totals_set[d] = totals[...]
    tot_start, tot_wait, tot_end = exchange(
        lambda peer: totals, lambda me: totals_set.at[me], tot_send, tot_recv, "dp"
    )
    tot_start()
    piece = 256 if width >= 256 else width
    for n in range(0, width, piece):
        comb[:, n : n + piece] = dot(h_mat[...], s_col[:, n : n + piece])
    loop(0, columns, turn)
    tot_wait()

    scale_s, scale_t = weight / total_s, weight / total_t

    def pairs(b, carry):
        squares, divergence = carry
        value = sim_s[b]
        gap = value - sim_t[:, lanes_of(b)]
        their = facts_set[b, 2:3, :]
        student_part = exp_s[b] * (scale_s + their * totals_set[b, 0:1, :])
        teacher_part = exp_t[b] * (scale_t + their * facts_set[b, 1:2, :])
        pair = (2.0 * SIMILARITY_COEF / set_count) * gap * (weight + their) + INVERSE_TEMP * (
            student_part - teacher_part
        )
        w_mat[:, lanes_of(b)] = (pair * facts_set[b, 0:1, :]).astype(BF16)
        return squares + gap * gap, divergence + exp_t[b] * gap

    squares, divergence = lax.fori_loop(0, columns, pairs, (zero, zero))
    for n in range(0, width, piece):
        comb[:, n : n + piece] += dot(w_mat[...], s_set[:, n : n + piece])
    combined = comb[...] * LOSS_SCALE
    inner = jnp.sum(back[...] * combined, 1, keepdims=True) - LOSS_SCALE * weight * cosine
    split_store(
        combined * inverse
        - s_set[rows_of(d)].astype(F32) * (inner * inverse * inverse * inverse)
    )
    teacher_scale = LOSS_SCALE * weight * inverse

    def gradient(q):
        both = dot(pair_rows[...], proj[:, chunk_of(q)])
        value = both[0:rows] + both[rows : 2 * rows] - teacher_scale * unit_t[q].astype(F32)
        grad[q] = value.astype(BF16)

    def grad_copy(o):
        peer = lax.rem(d + o, columns)
        return copy(
            grad.at[peer], grad_cols.at[rows_of(d)], grad_send.at[o], grad_recv.at[o], g, peer
        )

    def gradient_step(o):
        gradient(lax.rem(d + o, columns))
        grad_copy(o).start()

    loop(1, columns, gradient_step)
    gradient(d)
    grad_cols[rows_of(d)] = grad[d]

    sim_term = (SIMILARITY_COEF / set_count) * jnp.sum(squares, 1, keepdims=True)
    kl_term = (
        jnp.log(total_s)
        - jnp.log(total_t)
        - INVERSE_TEMP * jnp.sum(divergence, 1, keepdims=True) / total_t
    )
    per_text = weight * (1.0 - cosine * inverse + sim_term + kl_term) + jnp.sum(
        hard_loss, 1, keepdims=True
    )
    loss_tile[...] = jnp.broadcast_to(jnp.sum(per_text, 0, keepdims=True), loss_tile.shape)
    loss_set[d] = loss_tile[...]
    lset_start, lset_wait, lset_end = exchange(
        lambda peer: loss_tile, lambda me: loss_set.at[me], lset_send, lset_recv, "dp"
    )
    lset_start()

    comb[...] = jnp.zeros_like(comb)

    def student_part(q):
        comb[...] += dot_t(grad[q], proj[:, chunk_of(q)])

    loop(0, count, student_part)
    student_out[...] = comb[...].astype(BF16)

    lset_wait()
    loss_tile2[...] = jnp.sum(loss_set[...], 0)
    loss_col[g] = loss_tile2[...]
    lcol_start, lcol_wait, lcol_end = exchange(
        lambda peer: loss_tile2, lambda me: loss_col.at[me], lcol_send, lcol_recv, "group"
    )
    lcol_start()

    def grad_arrive(o):
        source = lax.rem(d + columns - o, columns)
        place = grad_cols.at[rows_of(source)]
        copy(place, place, grad_send.at[o], grad_recv.at[o], g, source).wait_recv()

    loop(1, columns, grad_arrive)
    share = width // groups
    for n in range(0, width, piece):
        result = dot(s_turned[n : n + piece, :], grad_cols[...]).astype(BF16)
        for i in range(piece // share):
            within[n // share + i] = result[i * share : (i + 1) * share]
    out_start, out_wait, out_end = exchange(
        lambda peer: within.at[peer], lambda me: arrived.at[me], out_send, out_recv, "group"
    )
    out_start()
    arrived[g] = within[g]
    lcol_wait()
    loss_out[0, 0] = jnp.sum(loss_col[...]) * (
        1.0 / (8.0 * 128.0 * rows * groups * columns)
    )
    out_wait()
    projector_out[...] = jnp.sum(arrived[...].astype(F32), 0)

    for _, one in pending:
        one.wait_send()
    loop(1, columns, lambda o: grad_copy(o).wait_send())
    for end in (unit_end, fcol_end, fset_end, part_end, tot_end, lset_end, lcol_end, out_end):
        end()


def local_program(
    student, teacher, teacher_similarity, projector, hard_group, hard_local, hard_count, text_weight
):
    rows, width = student.shape
    groups = lax.axis_size("group")
    columns = lax.axis_size("dp")
    wide = projector.shape[1]
    chunk = wide // groups
    dma = pltpu.SemaphoreType.DMA
    vm = pltpu.VMEM
    texts, col_texts = rows * columns, rows * groups
    scratch = [
        vm((texts, width), BF16),
        vm((col_texts, width), BF16),
        vm((width, texts), BF16),
        vm((width, wide), BF16),
        vm((rows, wide), BF16),
        vm((rows, texts), F32),
        vm((groups, rows, chunk), BF16),
        vm((col_texts, chunk), BF16),
        vm((columns, rows, rows), F32),
        vm((columns, rows, rows), F32),
        vm((columns, rows, rows), F32),
        vm((rows, rows), F32),
        vm((rows, col_texts), BF16),
        vm((rows, texts), BF16),
        vm((rows, width), F32),
        vm((rows, width), F32),
        vm((2 * rows, width), BF16),
        vm((groups, rows, chunk), BF16),
        vm((texts, chunk), BF16),
        vm((8, rows), F32),
        vm((columns, 8, rows), F32),
        vm((groups, 8, rows), F32),
        vm((HARD * groups, rows), F32),
        vm((groups, HARD * groups, rows), F32),
        vm((HARD * groups, rows), F32),
        vm((8, rows), F32),
        vm((columns, 8, rows), F32),
        vm((groups, width // groups, chunk), BF16),
        vm((groups, width // groups, chunk), BF16),
        vm((8, 128), F32),
        vm((columns, 8, 128), F32),
        vm((8, 128), F32),
        vm((groups, 8, 128), F32),
        dma((5,)),
        dma((2 * columns + 2,)),
        dma((2 * columns,)),
        dma((2 * groups,)),
        dma((2 * groups,)),
    ] + [dma((groups,)) for _ in range(18)]
    anywhere = pl.BlockSpec(memory_space=pl.ANY)
    vmem = pl.BlockSpec(memory_space=pltpu.VMEM)
    loss, student_gradient, projector_gradient = pl.pallas_call(
        functools.partial(kernel, groups, columns),
        out_shape=(
            jax.ShapeDtypeStruct((1, 1), F32),
            jax.ShapeDtypeStruct((rows, width), BF16),
            jax.ShapeDtypeStruct((width // groups, wide // columns), F32),
        ),
        in_specs=[anywhere] * 4 + [vmem] * 4,
        out_specs=(pl.BlockSpec(memory_space=pltpu.SMEM), vmem, vmem),
        scratch_shapes=scratch,
        compiler_params=pltpu.CompilerParams(
            collective_id=0, has_side_effects=True, vmem_limit_bytes=58 * 1024 * 1024
        ),
        cost_estimate=pl.CostEstimate(
            flops=12_000_000_000, bytes_accessed=16_000_000, transcendentals=1_000_000
        ),
    )(
        student,
        teacher,
        teacher_similarity,
        projector,
        hard_group.T,
        hard_local.T,
        hard_count.reshape(1, rows),
        text_weight.reshape(1, rows),
    )
    return loss.reshape(()), student_gradient, projector_gradient


def solution(mesh):
    return jax.shard_map(
        local_program,
        mesh=mesh,
        in_specs=(
            P(("group", "dp"), None),
            P(("group", "dp"), None),
            P(("group", "dp"), None),
            P(),
            P(("group", "dp"), None),
            P(("group", "dp"), None),
            P(("group", "dp")),
            P(("group", "dp")),
        ),
        out_specs=(P(), P(("group", "dp"), None), P("group", "dp")),
        check_vma=False,
    )
```

time: 331 us -> 129 us (0.39)
  blocking collectives: 253 us -> 0 us
  Pallas kernels: 0 us -> 123 us
  matrix products: 38.7 us -> 0 us
  between operations: 17.7 us -> 2.33 us
  starting transfers between devices: 8.55 us -> 0 us
  other arithmetic: 5.34 us -> 0 us
    psum x2 -> x0, blocking collectives: 147 us -> none  [the longest x1 87 us: local(): lax.psum(local_loss, ('group', 'dp')) / (rows * groups * columns)]
    pallas_call x0 -> x1, Pallas kernels: none -> 123 us  [local_program(): pl.pallas_call(functools.partial(kernel, groups, columns), out_shape=(jax...]
    all_gather x3 -> x0, blocking collectives: 88.1 us -> none  [the longest x1 34.3 us: local(): facts_set = lax.all_gather(facts[:3], 'dp', axis=1, tiled=True)]
    dot_general x10 -> x0, matrix products: 38.7 us -> none  [the longest x5 25.8 us: dot_t(): lax.dot_general(left, right, (((1,), (1,)), ((), ())), preferred_element_...]
    all_to_all x1 -> x0, blocking collectives: 18.5 us -> none  [local(): lax.all_to_all(proj_gradient, 'dp', split_axis=1, concat_axis=0, tiled=True)]
    all_to_all x1 -> x0, starting transfers between devices: 8.44 us -> none  [local(): lax.all_to_all(teacher_unit, 'group', split_axis=1, concat_axis=0, tiled=...]
    reduce_sum x4 -> x0, other arithmetic: 3.95 us -> none  [the longest x1 1.52 us: row_norms(): return jnp.sqrt(jnp.sum(values * values, 1, keepdims=True) + EPSILON)]
  transfers between devices with their start and end apart: 4 -> 0, of which waited for: 0 -> 0; matrix products, arithmetic and copies ran while one was open for 10% -> 0% of each run, Pallas kernels for 0% -> 0%
where the time goes in v2:
time: 129 us
  Pallas kernels  123 us (95%)
  local copies, waits for them, and re-layouts  3.14 us (2%)
  between operations  2.33 us (2%)
    pallas_call x1, Pallas kernels, local_program(): pl.pallas_call(functools.partial(kernel, groups, columns), out_shape=(jax...  123 us
    unnamed x2, local copies, waits for them, and re-layouts  3.14 us

profile of v2, /device:TPU:1, one launch (start us, length us, event | category | flops | bytes accessed | tf_op | source)
XLA Modules:
  0.0 128.7 jit_solution(7551251401640946626)
XLA Ops:
  0.6 123.2 %shard_map.103 = (f32[1,1]{1,0:T(1,128)}, bf16[128,1024]{1,0:T(8,128)(2,1)}, f32[64,256]{1,0:T(8,128)}) custom-call(bf16[128,1024]{1,0:T(8,128)(2,1)} %student.1, bf16[128,4096]{1,0:T(8,128)(2,1)} %teacher.1, f32[128,2048]{1,0:T(8,128)} %sims.1, bf16[1024,4096]{1,0:T(8,128)(2,1)} %projector.1, s32[2,128]{1,0:T(2,128)} %bitcast.5, s32[2,128]{1,0:T(2,128)} %bitcast.6, ...), custom_call_target="tpu_custom_call" | custom-call | flops 12000000000 | bytes 16000000 | tf_op jit(solution)/shard_map/pallas_call | solution.py:638
  124.4 1.7 %copy.15 = bf16[128,1024]{1,0:T(8,128)(2,1)} copy(bf16[128,1024]{1,0:T(8,128)(2,1)} %get-tuple-element.13) | data formatting | bytes 524288
  126.1 1.5 %copy.16 = f32[64,256]{1,0:T(8,128)} copy(f32[64,256]{1,0:T(8,128)} %get-tuple-element.14) | data formatting | bytes 131072

commit v3 on v2

--- a/solution.py
+++ b/solution.py
@@ -50,6 +50,7 @@
     s_set,
     s_col,
     s_turned,
+    c_turned,
     proj,
     teach,
     sim_t,
@@ -58,6 +59,7 @@
     sim_s,
     exp_s,
     exp_t,
+    cross_s,
     row_total,
     h_mat,
     w_mat,
@@ -76,6 +78,8 @@
     totals_set,
     within,
     arrived,
+    mirror_out,
+    mirror_in,
     loss_tile,
     loss_set,
     loss_tile2,
@@ -103,6 +107,7 @@
     lset_recv,
     lcol_send,
     lcol_recv,
+    mirror_sem,
 ):
     rows, width = student.shape
     chunk = unit_t.shape[2]
@@ -164,7 +169,27 @@
         )
 
     loop(1, columns, greet)
-    pl.semaphore_wait(barrier, 2 * (columns - 1))
+
+    @pl.when(g != d)
+    def greet_mirror():
+        pl.semaphore_signal(barrier, inc=1, device_id=(d, g), device_id_type=MESH)
+
+    local[2].wait()
+
+    def square_sum(q, total):
+        t = teach[:, chunk_of(q)].astype(F32)
+        t = t * t
+        return total + sum(t[:, i : i + 128] for i in range(0, chunk, 128))
+
+    t_total = lax.fori_loop(0, count, square_sum, jnp.zeros((rows, 128), F32))
+    t_scale = 1.0 / jnp.sqrt(jnp.sum(t_total, 1, keepdims=True) + EPSILON)
+
+    def make_unit(q):
+        unit_t[q] = (teach[:, chunk_of(q)].astype(F32) * t_scale).astype(BF16)
+
+    loop(0, count, make_unit)
+    others = (lax.rem(g - d + groups, groups) + groups - 1) // groups
+    pl.semaphore_wait(barrier, 2 * (columns - 1) + others)
 
     pending = []
 
@@ -280,20 +305,6 @@
             lambda: loop(1, size, lambda o: at(o).wait_send()),
         )
 
-    local[2].wait()
-
-    def square_sum(q, total):
-        t = teach[:, chunk_of(q)].astype(F32)
-        t = t * t
-        return total + sum(t[:, i : i + 128] for i in range(0, chunk, 128))
-
-    t_total = lax.fori_loop(0, count, square_sum, jnp.zeros((rows, 128), F32))
-    t_scale = 1.0 / jnp.sqrt(jnp.sum(t_total, 1, keepdims=True) + EPSILON)
-
-    def make_unit(q):
-        unit_t[q] = (teach[:, chunk_of(q)].astype(F32) * t_scale).astype(BF16)
-
-    loop(0, count, make_unit)
     unit_start, unit_wait, unit_end = exchange(
         lambda peer: unit_t.at[peer], lambda me: cols_t.at[rows_of(me)], unit_send, unit_recv, "group"
     )
@@ -329,7 +340,6 @@
 
     split_store(back[...] * inverse)
     pass_set(0)
-    pass_col(0)
 
     sub = lax.broadcasted_iota(jnp.int32, (rows, rows), 0)
     lane = lax.broadcasted_iota(jnp.int32, (rows, rows), 1)
@@ -374,59 +384,106 @@
     fcol_start()
     fset_start()
     pass_set(1)
-    pass_col(1)
+    pass_col(0)
 
     row_total[...] = zero
 
-    def similarity(block):
+    def multiply(block):
         both = dot_t(pair_rows[...], s_set[rows_of(block)])
-        value = (both[0:rows] + both[rows : 2 * rows]) * facts_set[block, 0:1, :]
+        sim_s[block] = both[0:rows] + both[rows : 2 * rows]
+        s_turned[:, lanes_of(block)] = s_set[rows_of(block)].T
+
+    def finish(block):
+        value = sim_s[block] * facts_set[block, 0:1, :]
         grown = jnp.exp(value * INVERSE_TEMP)
         grown = jnp.where(jnp.logical_and(eye, block == d), 0.0, grown)
         sim_s[block] = value
         exp_s[block] = grown
         row_total[...] += grown
 
-    def turn(block):
-        s_turned[:, lanes_of(block)] = s_set[rows_of(block)].T
+    for fy, dz in ((0, 0), (1, 0), (0, -1), (0, 1), (1, -1), (1, 1)):
+        multiply(set_id(fy, dz))
+    pass_set(2)
+    pass_col(1)
+    for fy, dz in ((0, -2), (0, 2), (1, -2), (1, 2)):
+        multiply(set_id(fy, dz))
 
     unit_wait()
     fcol_wait()
-    step_rows = 512 if groups * rows >= 512 else groups * rows
-    numbers = lax.broadcasted_iota(jnp.int32, (step_rows, rows), 0).astype(F32)
+    numbers = lax.broadcasted_iota(jnp.int32, (rows, 2 * rows), 0).astype(F32)
+    step_blocks = 4
 
     def pick(b):
-        queries = cols_t[rows_of(b)]
-        sums = [jnp.zeros((1, rows), F32)] * HARD
-        for c in range(0, groups * rows, step_rows):
-            gram = dot_t(cols_t[c : c + step_rows], queries)
-            for k in range(HARD):
-                wanted = facts_col[b, 3 + k : 4 + k, :] - float(c)
-                sums[k] = sums[k] + jnp.sum(
-                    jnp.where(numbers == wanted, gram, 0.0), 0, keepdims=True
+        queries = cols_t[pl.ds(pl.multiple_of(2 * b * rows, 2 * rows), 2 * rows)]
+        first, second = [
+            jnp.concatenate([facts_col[2 * b + i, 3 + k : 4 + k, :] for i in (0, 1)], 1)
+            for k in range(HARD)
+        ]
+        sums = [jnp.zeros((1, 2 * rows), F32)] * HARD
+        for c in range(0, groups, step_blocks):
+            gram = dot_t(cols_t[c * rows : (c + step_blocks) * rows], queries)
+            for j in range(step_blocks):
+                low = float((c + j) * rows)
+                here = jnp.logical_and(first >= low, first < low + rows)
+                wanted = jnp.where(here, first, second) - low
+                found = jnp.sum(
+                    jnp.where(numbers == wanted, gram[j * rows : (j + 1) * rows], 0.0),
+                    0,
+                    keepdims=True,
                 )
+                sums[0] = sums[0] + jnp.where(here, found, 0.0)
+                sums[1] = sums[1] + jnp.where(here, 0.0, found)
         for k in range(HARD):
-            part[pl.ds(k * groups + b, 1), :] = sums[k]
-
-    loop(0, groups, pick)
+            for i in (0, 1):
+                part[pl.ds(k * groups + 2 * b + i, 1), :] = sums[k][:, i * rows : (i + 1) * rows]
+
+    loop(0, groups // 4, pick)
+    pass_set(3)
+    pass_col(2)
+    loop(groups // 4, groups // 2, pick)
     part_start, part_wait, part_end = exchange(
         lambda peer: part, lambda me: parts.at[me], part_send, part_recv, "group"
     )
     part_start()
     parts[g] = part[...]
-    pass_set(2)
-    pass_col(2)
-
+    for fy, dz in ((0, -3), (0, 3), (1, -3), (1, 3)):
+        multiply(set_id(fy, dz))
     fset_wait()
-    for fy, dz in ((0, 0), (1, 0), (0, -1), (0, 1), (1, -1), (1, 1)):
-        similarity(set_id(fy, dz))
-    pass_set(3)
-    for fy, dz in ((0, -2), (0, 2), (1, -2), (1, 2)):
-        similarity(set_id(fy, dz))
-
+
+    def finish_near(i):
+        fy, dz = i // (zs - 1), lax.rem(i, zs - 1) - (zs // 2 - 1)
+        finish((yl + fy - 2 * fy * yl) * zs + lax.rem(z + dz + zs, zs))
+
+    loop(0, 2 * (zs - 1), finish_near)
     for dx in range(xs):
         for fy in (0, 1):
             wait_col(dx, fy, 1)
+
+    def cross_pair(b):
+        both = dot_t(
+            pair_rows[...], s_col[pl.ds(pl.multiple_of(2 * b * rows, 2 * rows), 2 * rows)]
+        )
+        value = both[0:rows] + both[rows : 2 * rows]
+        for i in (0, 1):
+            cross_s[2 * b + i] = (
+                value[:, i * rows : (i + 1) * rows] * facts_col[2 * b + i, 0:1, :]
+            )
+
+    loop(0, groups // 2, cross_pair)
+    for fy in (0, 1):
+        wait_set(fy, zs // 2, 0)
+        wait_set(fy, zs // 2, 1)
+        far = set_id(fy, zs // 2)
+        multiply(far)
+        finish(far)
+    total_s = jnp.sum(row_total[...], 1, keepdims=True)
+    totals[...] = jnp.broadcast_to(to_row(1.0 / total_s), totals.shape)
+    totals_set[d] = totals[...]
+    tot_start, tot_wait, tot_end = exchange(
+        lambda peer: totals, lambda me: totals_set.at[me], tot_send, tot_recv, "dp"
+    )
+    tot_start()
+
     part_wait()
     hard_sum[...] = jnp.sum(parts[...], 0)
     weight = to_column(weight_row)
@@ -437,9 +494,8 @@
     lane_ids = lane.astype(F32)
 
     def hard(b, loss):
-        both = dot_t(pair_rows[...], s_col[rows_of(b)])
         scale = facts_col[b, 0:1, :]
-        cross = (both[0:rows] + both[rows : 2 * rows]) * scale
+        cross = cross_s[b]
         ids = lane_ids + (b * rows).astype(F32)
         value = jnp.zeros_like(cross)
         for k in range(HARD):
@@ -455,42 +511,31 @@
         return loss
 
     hard_loss = lax.fori_loop(0, groups, hard, zero)
-    for fy, dz in ((0, -3), (0, 3), (1, -3), (1, 3)):
-        similarity(set_id(fy, dz))
-    for fy in (0, 1):
-        wait_set(fy, zs // 2, 0)
-        wait_set(fy, zs // 2, 1)
-        similarity(set_id(fy, zs // 2))
-
-    total_s = jnp.sum(row_total[...], 1, keepdims=True)
-    totals[...] = jnp.broadcast_to(to_row(1.0 / total_s), totals.shape)
-    totals_set[d] = totals[...]
-    tot_start, tot_wait, tot_end = exchange(
-        lambda peer: totals, lambda me: totals_set.at[me], tot_send, tot_recv, "dp"
-    )
-    tot_start()
     piece = 256 if width >= 256 else width
     for n in range(0, width, piece):
         comb[:, n : n + piece] = dot(h_mat[...], s_col[:, n : n + piece])
-    loop(0, columns, turn)
-    tot_wait()
-
     scale_s, scale_t = weight / total_s, weight / total_t
 
     def pairs(b, carry):
         squares, divergence = carry
-        value = sim_s[b]
-        gap = value - sim_t[:, lanes_of(b)]
+        gap = sim_s[b] - sim_t[:, lanes_of(b)]
         their = facts_set[b, 2:3, :]
-        student_part = exp_s[b] * (scale_s + their * totals_set[b, 0:1, :])
-        teacher_part = exp_t[b] * (scale_t + their * facts_set[b, 1:2, :])
-        pair = (2.0 * SIMILARITY_COEF / set_count) * gap * (weight + their) + INVERSE_TEMP * (
-            student_part - teacher_part
-        )
-        w_mat[:, lanes_of(b)] = (pair * facts_set[b, 0:1, :]).astype(BF16)
-        return squares + gap * gap, divergence + exp_t[b] * gap
+        grown = exp_t[b]
+        sim_s[b] = (2.0 * SIMILARITY_COEF / set_count) * gap * (
+            weight + their
+        ) + INVERSE_TEMP * (exp_s[b] * scale_s - grown * (scale_t + their * facts_set[b, 1:2, :]))
+        return squares + gap * gap, divergence + grown * gap
 
     squares, divergence = lax.fori_loop(0, columns, pairs, (zero, zero))
+    tot_wait()
+
+    def complete(b):
+        their = INVERSE_TEMP * facts_set[b, 2:3, :] * totals_set[b, 0:1, :]
+        w_mat[:, lanes_of(b)] = (
+            (sim_s[b] + exp_s[b] * their) * facts_set[b, 0:1, :]
+        ).astype(BF16)
+
+    loop(0, columns, complete)
     for n in range(0, width, piece):
         comb[:, n : n + piece] += dot(w_mat[...], s_set[:, n : n + piece])
     combined = comb[...] * LOSS_SCALE
@@ -499,26 +544,53 @@
         combined * inverse
         - s_set[rows_of(d)].astype(F32) * (inner * inverse * inverse * inverse)
     )
+    thin = chunk // 2
     teacher_scale = LOSS_SCALE * weight * inverse
 
     def gradient(q):
         both = dot(pair_rows[...], proj[:, chunk_of(q)])
         value = both[0:rows] + both[rows : 2 * rows] - teacher_scale * unit_t[q].astype(F32)
-        grad[q] = value.astype(BF16)
-
-    def grad_copy(o):
+        for h in (0, 1):
+            grad[h, q] = value[:, h * thin : (h + 1) * thin].astype(BF16)
+
+    def set_copy(o):
         peer = lax.rem(d + o, columns)
         return copy(
-            grad.at[peer], grad_cols.at[rows_of(d)], grad_send.at[o], grad_recv.at[o], g, peer
+            grad.at[0, peer],
+            grad_cols.at[0, rows_of(d)],
+            grad_send.at[0, o],
+            grad_recv.at[0, o],
+            g,
+            peer,
+        )
+
+    def col_copy(o):
+        peer = lax.rem(g + o, groups)
+        return copy(
+            grad.at[1, peer],
+            grad_cols.at[1, rows_of(g)],
+            grad_send.at[1, o],
+            grad_recv.at[1, o],
+            peer,
+            d,
         )
 
     def gradient_step(o):
-        gradient(lax.rem(d + o, columns))
-        grad_copy(o).start()
-
-    loop(1, columns, gradient_step)
-    gradient(d)
-    grad_cols[rows_of(d)] = grad[d]
+        q = lax.rem(d + o, columns)
+        gradient(q)
+        apart = lax.rem(q + groups - g, groups)
+
+        @pl.when(apart != 0)
+        def send_col_part():
+            col_copy(apart).start()
+
+        @pl.when(o != columns)
+        def send_set_part():
+            set_copy(o).start()
+
+    loop(1, columns + 1, gradient_step)
+    grad_cols[0, rows_of(d)] = grad[0, d]
+    grad_cols[1, rows_of(g)] = grad[1, g]
 
     sim_term = (SIMILARITY_COEF / set_count) * jnp.sum(squares, 1, keepdims=True)
     kl_term = (
@@ -536,14 +608,57 @@
     )
     lset_start()
 
+    def turn_col(b):
+        c_turned[:, lanes_of(b)] = s_col[rows_of(b)].T
+
+    loop(0, groups, turn_col)
+
+    def set_arrive(o):
+        source = lax.rem(d + columns - o, columns)
+        place = grad_cols.at[0, rows_of(source)]
+        copy(place, place, grad_send.at[0, o], grad_recv.at[0, o], g, source).wait_recv()
+
+    def col_arrive(o):
+        source = lax.rem(g + groups - o, groups)
+        place = grad_cols.at[1, rows_of(source)]
+        copy(place, place, grad_send.at[1, o], grad_recv.at[1, o], source, d).wait_recv()
+
+    share = width // groups
+
+    def products(h, turned):
+        for n in range(0, width, piece):
+            result = dot(turned[n : n + piece, :], grad_cols[h]).astype(BF16)
+            for i in range(piece // share):
+                within[h, n // share + i] = result[i * share : (i + 1) * share]
+
+    def out_exchange(h, along):
+        return exchange(
+            lambda peer: within.at[h, peer],
+            lambda me: arrived.at[h, me],
+            out_send.at[h],
+            out_recv.at[h],
+            along,
+        )
+
+    loop(1, groups, col_arrive)
+    products(1, c_turned)
+    out1_start, out1_wait, out1_end = out_exchange(1, "dp")
+    out1_start()
+    arrived[1, d] = within[1, d]
+
     comb[...] = jnp.zeros_like(comb)
 
     def student_part(q):
-        comb[...] += dot_t(grad[q], proj[:, chunk_of(q)])
+        both = jnp.concatenate([grad[0, q], grad[1, q]], 1)
+        comb[...] += dot_t(both, proj[:, chunk_of(q)])
 
     loop(0, count, student_part)
     student_out[...] = comb[...].astype(BF16)
 
+    for _, one in pending:
+        one.wait_send()
+    for end in (unit_end, fcol_end, fset_end, part_end, tot_end):
+        end()
     lset_wait()
     loss_tile2[...] = jnp.sum(loss_set[...], 0)
     loss_col[g] = loss_tile2[...]
@@ -552,33 +667,38 @@
     )
     lcol_start()
 
-    def grad_arrive(o):
-        source = lax.rem(d + columns - o, columns)
-        place = grad_cols.at[rows_of(source)]
-        copy(place, place, grad_send.at[o], grad_recv.at[o], g, source).wait_recv()
-
-    loop(1, columns, grad_arrive)
-    share = width // groups
-    for n in range(0, width, piece):
-        result = dot(s_turned[n : n + piece, :], grad_cols[...]).astype(BF16)
-        for i in range(piece // share):
-            within[n // share + i] = result[i * share : (i + 1) * share]
-    out_start, out_wait, out_end = exchange(
-        lambda peer: within.at[peer], lambda me: arrived.at[me], out_send, out_recv, "group"
-    )
-    out_start()
-    arrived[g] = within[g]
+    loop(1, columns, set_arrive)
+    products(0, s_turned)
+    out0_start, out0_wait, out0_end = out_exchange(0, "group")
+    out0_start()
+    arrived[0, g] = within[0, g]
+    out1_wait()
+    mirror_out[...] = jnp.sum(arrived[1].astype(F32), 0)
+    mirror = copy(mirror_out, mirror_in, mirror_sem.at[0], mirror_sem.at[1], d, g)
+
+    @pl.when(g != d)
+    def send_mirror():
+        mirror.start()
+
     lcol_wait()
     loss_out[0, 0] = jnp.sum(loss_col[...]) * (
         1.0 / (8.0 * 128.0 * rows * groups * columns)
     )
-    out_wait()
-    projector_out[...] = jnp.sum(arrived[...].astype(F32), 0)
-
-    for _, one in pending:
-        one.wait_send()
-    loop(1, columns, lambda o: grad_copy(o).wait_send())
-    for end in (unit_end, fcol_end, fset_end, part_end, tot_end, lset_end, lcol_end, out_end):
+    out0_wait()
+    projector_out[:, :thin] = jnp.sum(arrived[0].astype(F32), 0)
+
+    @pl.when(g != d)
+    def take_mirror():
+        mirror.wait()
+        projector_out[:, thin:] = mirror_in[...]
+
+    @pl.when(g == d)
+    def keep_own():
+        projector_out[:, thin:] = mirror_out[...]
+
+    loop(1, columns, lambda o: set_copy(o).wait_send())
+    loop(1, groups, lambda o: col_copy(o).wait_send())
+    for end in (lset_end, lcol_end, out0_end, out1_end):
         end()
 
 
@@ -597,6 +717,7 @@
         vm((texts, width), BF16),
         vm((col_texts, width), BF16),
         vm((width, texts), BF16),
+        vm((width, col_texts), BF16),
         vm((width, wide), BF16),
         vm((rows, wide), BF16),
         vm((rows, texts), F32),
@@ -605,14 +726,15 @@
         vm((columns, rows, rows), F32),
         vm((columns, rows, rows), F32),
         vm((columns, rows, rows), F32),
+        vm((groups, rows, rows), F32),
         vm((rows, rows), F32),
         vm((rows, col_texts), BF16),
         vm((rows, texts), BF16),
         vm((rows, width), F32),
         vm((rows, width), F32),
         vm((2 * rows, width), BF16),
-        vm((groups, rows, chunk), BF16),
-        vm((texts, chunk), BF16),
+        vm((2, columns, rows, chunk // 2), BF16),
+        vm((2, texts, chunk // 2), BF16),
         vm((8, rows), F32),
         vm((columns, 8, rows), F32),
         vm((groups, 8, rows), F32),
@@ -621,8 +743,10 @@
         vm((HARD * groups, rows), F32),
         vm((8, rows), F32),
         vm((columns, 8, rows), F32),
-        vm((groups, width // groups, chunk), BF16),
-        vm((groups, width // groups, chunk), BF16),
+        vm((2, groups, width // groups, chunk // 2), BF16),
+        vm((2, groups, width // groups, chunk // 2), BF16),
+        vm((width // groups, chunk // 2), F32),
+        vm((width // groups, chunk // 2), F32),
         vm((8, 128), F32),
         vm((columns, 8, 128), F32),
         vm((8, 128), F32),
@@ -632,7 +756,7 @@
         dma((2 * columns,)),
         dma((2 * groups,)),
         dma((2 * groups,)),
-    ] + [dma((groups,)) for _ in range(18)]
+    ] + [dma((2, groups) if i in (10, 11, 12, 13) else (groups,)) for i in range(18)] + [dma((2,))]
     anywhere = pl.BlockSpec(memory_space=pl.ANY)
     vmem = pl.BlockSpec(memory_space=pltpu.VMEM)
     loss, student_gradient, projector_gradient = pl.pallas_call(

time: 129 us -> 112 us (0.87)
  Pallas kernels: 123 us -> 106 us
    pallas_call x1, Pallas kernels: 123 us -> 106 us  [local_program(): pl.pallas_call(functools.partial(kernel, groups, columns), out_shape=(jax...]
where the time goes in v3:
time: 112 us; the launch traced here: 111 us
  Pallas kernels  106 us (95%)
  local copies, waits for them, and re-layouts  3.14 us (3%)
  between operations  2.33 us (2%)
    pallas_call x1, Pallas kernels, local_program(): pl.pallas_call(functools.partial(kernel, groups, columns), out_shape=(jax...  106 us
    unnamed x2, local copies, waits for them, and re-layouts  3.14 us

profile of v3, /device:TPU:1, one launch (start us, length us, event | category | flops | bytes accessed | tf_op | source)
XLA Modules:
  0.0 111.5 jit_solution(11297398456989046395)
XLA Ops:
  0.6 106.0 %shard_map.103 = (f32[1,1]{1,0:T(1,128)}, bf16[128,1024]{1,0:T(8,128)(2,1)}, f32[64,256]{1,0:T(8,128)}) custom-call(bf16[128,1024]{1,0:T(8,128)(2,1)} %student.1, bf16[128,4096]{1,0:T(8,128)(2,1)} %teacher.1, f32[128,2048]{1,0:T(8,128)} %sims.1, bf16[1024,4096]{1,0:T(8,128)(2,1)} %projector.1, s32[2,128]{1,0:T(2,128)} %bitcast.5, s32[2,128]{1,0:T(2,128)} %bitcast.6, ...), custom_call_target="tpu_custom_call" | custom-call | flops 12000000000 | bytes 16000000 | tf_op jit(solution)/shard_map/pallas_call | solution.py:762
  107.2 1.7 %copy.15 = bf16[128,1024]{1,0:T(8,128)(2,1)} copy(bf16[128,1024]{1,0:T(8,128)(2,1)} %get-tuple-element.13) | data formatting | bytes 524288
  108.9 1.5 %copy.16 = f32[64,256]{1,0:T(8,128)} copy(f32[64,256]{1,0:T(8,128)} %get-tuple-element.14) | data formatting | bytes 131072

commit v4 on v3

--- a/solution.py
+++ b/solution.py
@@ -40,13 +40,18 @@
     teacher,
     sims,
     projector,
+    hard_group_in,
+    hard_local_in,
+    hard_count_in,
+    text_weight_in,
+    loss_out,
+    student_out,
+    projector_out,
     hard_group,
     hard_local,
     hard_count,
     text_weight,
-    loss_out,
-    student_out,
-    projector_out,
+    student_made,
     s_set,
     s_col,
     s_turned,
@@ -154,8 +159,12 @@
         pltpu.make_async_copy(teacher, teach, local_sem.at[2]),
         pltpu.make_async_copy(projector, proj, local_sem.at[3]),
         pltpu.make_async_copy(sims, sim_t, local_sem.at[4]),
+        pltpu.make_async_copy(hard_group_in, hard_group, local_sem.at[5]),
+        pltpu.make_async_copy(hard_local_in, hard_local, local_sem.at[6]),
+        pltpu.make_async_copy(hard_count_in, hard_count, local_sem.at[7]),
+        pltpu.make_async_copy(text_weight_in, text_weight, local_sem.at[8]),
     ]
-    for one in (2, 0, 1, 3, 4):
+    for one in (2, 0, 1, 3, 4, 5, 6, 7, 8):
         local[one].start()
 
     barrier = pltpu.get_barrier_semaphore()
@@ -300,7 +309,7 @@
             copy(dst(source), dst(source), send.at[o], recv.at[o], *where).wait_recv()
 
         return (
-            lambda: loop(1, size, lambda o: at(o).start()),
+            lambda: loop(1, size, lambda o: at(lax.rem(5 * o, size)).start()),
             lambda: loop(1, size, arrive),
             lambda: loop(1, size, lambda o: at(o).wait_send()),
         )
@@ -351,7 +360,8 @@
     def to_column(row):
         return jnp.sum(jnp.where(eye, row, 0.0), 1, keepdims=True)
 
-    local[4].wait()
+    for one in range(4, 9):
+        local[one].wait()
 
     def teacher_exp(b, total):
         value = jnp.exp(sim_t[:, lanes_of(b)] * INVERSE_TEMP)
@@ -576,7 +586,8 @@
         )
 
     def gradient_step(o):
-        q = lax.rem(d + o, columns)
+        turn = lax.rem(5 * o, columns)
+        q = lax.rem(d + turn, columns)
         gradient(q)
         apart = lax.rem(q + groups - g, groups)
 
@@ -586,7 +597,7 @@
 
         @pl.when(o != columns)
         def send_set_part():
-            set_copy(o).start()
+            set_copy(turn).start()
 
     loop(1, columns + 1, gradient_step)
     grad_cols[0, rows_of(d)] = grad[0, d]
@@ -653,7 +664,9 @@
         comb[...] += dot_t(both, proj[:, chunk_of(q)])
 
     loop(0, count, student_part)
-    student_out[...] = comb[...].astype(BF16)
+    student_made[...] = comb[...].astype(BF16)
+    student_copy = pltpu.make_async_copy(student_made, student_out, local_sem.at[9])
+    student_copy.start()
 
     for _, one in pending:
         one.wait_send()
@@ -684,6 +697,10 @@
     loss_out[0, 0] = jnp.sum(loss_col[...]) * (
         1.0 / (8.0 * 128.0 * rows * groups * columns)
     )
+    loop(1, columns, lambda o: set_copy(o).wait_send())
+    loop(1, groups, lambda o: col_copy(o).wait_send())
+    for end in (lset_end, lcol_end, out1_end):
+        end()
     out0_wait()
     projector_out[:, :thin] = jnp.sum(arrived[0].astype(F32), 0)
 
@@ -696,10 +713,8 @@
     def keep_own():
         projector_out[:, thin:] = mirror_out[...]
 
-    loop(1, columns, lambda o: set_copy(o).wait_send())
-    loop(1, groups, lambda o: col_copy(o).wait_send())
-    for end in (lset_end, lcol_end, out0_end, out1_end):
-        end()
+    out0_end()
+    student_copy.wait()
 
 
 def local_program(
@@ -714,6 +729,11 @@
     vm = pltpu.VMEM
     texts, col_texts = rows * columns, rows * groups
     scratch = [
+        vm((HARD, rows), jnp.int32),
+        vm((HARD, rows), jnp.int32),
+        vm((1, rows), jnp.int32),
+        vm((1, rows), F32),
+        vm((rows, width), BF16),
         vm((texts, width), BF16),
         vm((col_texts, width), BF16),
         vm((width, texts), BF16),
@@ -751,7 +771,7 @@
         vm((columns, 8, 128), F32),
         vm((8, 128), F32),
         vm((groups, 8, 128), F32),
-        dma((5,)),
+        dma((10,)),
         dma((2 * columns + 2,)),
         dma((2 * columns,)),
         dma((2 * groups,)),
@@ -766,8 +786,8 @@
             jax.ShapeDtypeStruct((rows, width), BF16),
             jax.ShapeDtypeStruct((width // groups, wide // columns), F32),
         ),
-        in_specs=[anywhere] * 4 + [vmem] * 4,
-        out_specs=(pl.BlockSpec(memory_space=pltpu.SMEM), vmem, vmem),
+        in_specs=[anywhere] * 8,
+        out_specs=(pl.BlockSpec(memory_space=pltpu.SMEM), anywhere, vmem),
         scratch_shapes=scratch,
         compiler_params=pltpu.CompilerParams(
             collective_id=0, has_side_effects=True, vmem_limit_bytes=58 * 1024 * 1024

time: 112 us -> 108 us (0.964)
  Pallas kernels: 106 us -> 103 us
    pallas_call x1, Pallas kernels: 106 us -> 103 us  [local_program(): pl.pallas_call(functools.partial(kernel, groups, columns), out_shape=(jax...]
where the time goes in v4:
time: 108 us
  Pallas kernels  103 us (95%)
  local copies, waits for them, and re-layouts  3.14 us (3%)
  between operations  2.33 us (2%)
    pallas_call x1, Pallas kernels, local_program(): pl.pallas_call(functools.partial(kernel, groups, columns), out_shape=(jax...  103 us
    unnamed x2, local copies, waits for them, and re-layouts  3.14 us

profile of v4, /device:TPU:1, one launch (start us, length us, event | category | flops | bytes accessed | tf_op | source)
XLA Modules:
  0.0 108.2 jit_solution(6019637803259378228)
XLA Ops:
  0.6 102.8 %shard_map.103 = (f32[1,1]{1,0:T(1,128)}, bf16[128,1024]{1,0:T(8,128)(2,1)}, f32[64,256]{1,0:T(8,128)}) custom-call(bf16[128,1024]{1,0:T(8,128)(2,1)} %student.1, bf16[128,4096]{1,0:T(8,128)(2,1)} %teacher.1, f32[128,2048]{1,0:T(8,128)} %sims.1, bf16[1024,4096]{1,0:T(8,128)(2,1)} %projector.1, s32[2,128]{1,0:T(2,128)} %bitcast.5, s32[2,128]{1,0:T(2,128)} %bitcast.6, ...), custom_call_target="tpu_custom_call" | custom-call | flops 12000000000 | bytes 16000000 | tf_op jit(solution)/shard_map/pallas_call | solution.py:782
  104.0 1.7 %copy.15 = bf16[128,1024]{1,0:T(8,128)(2,1)} copy(bf16[128,1024]{1,0:T(8,128)(2,1)} %get-tuple-element.13) | data formatting | bytes 524288
  105.6 1.5 %copy.16 = f32[64,256]{1,0:T(8,128)} copy(f32[64,256]{1,0:T(8,128)} %get-tuple-element.14) | data formatting | bytes 131072

commit v5 on v4

--- a/solution.py
+++ b/solution.py
@@ -153,6 +153,22 @@
             device_id_type=MESH,
         )
 
+    barrier = pltpu.get_barrier_semaphore()
+
+    def greet(o):
+        pl.semaphore_signal(
+            barrier, inc=1, device_id=(g, lax.rem(d + o, columns)), device_id_type=MESH
+        )
+        pl.semaphore_signal(
+            barrier, inc=1, device_id=(lax.rem(g + o, groups), d), device_id_type=MESH
+        )
+
+    loop(1, columns, greet)
+
+    @pl.when(g != d)
+    def greet_mirror():
+        pl.semaphore_signal(barrier, inc=1, device_id=(d, g), device_id_type=MESH)
+
     local = [
         pltpu.make_async_copy(student, s_set.at[rows_of(d)], local_sem.at[0]),
         pltpu.make_async_copy(student, s_col.at[rows_of(g)], local_sem.at[1]),
@@ -166,22 +182,6 @@
     ]
     for one in (2, 0, 1, 3, 4, 5, 6, 7, 8):
         local[one].start()
-
-    barrier = pltpu.get_barrier_semaphore()
-
-    def greet(o):
-        pl.semaphore_signal(
-            barrier, inc=1, device_id=(g, lax.rem(d + o, columns)), device_id_type=MESH
-        )
-        pl.semaphore_signal(
-            barrier, inc=1, device_id=(lax.rem(g + o, groups), d), device_id_type=MESH
-        )
-
-    loop(1, columns, greet)
-
-    @pl.when(g != d)
-    def greet_mirror():
-        pl.semaphore_signal(barrier, inc=1, device_id=(d, g), device_id_type=MESH)
 
     local[2].wait()
 

time: 108 us -> 109 us (level)
  no operation moved by 1% of the time
where the time goes in v5:
time: 109 us; the launch traced here: 108 us
  Pallas kernels  103 us (94%)
  local copies, waits for them, and re-layouts  3.14 us (3%)
  between operations  2.33 us (2%)
    pallas_call x1, Pallas kernels, local_program(): pl.pallas_call(functools.partial(kernel, groups, columns), out_shape=(jax...  103 us
    unnamed x2, local copies, waits for them, and re-layouts  3.14 us

profile of v5, /device:TPU:1, one launch (start us, length us, event | category | flops | bytes accessed | tf_op | source)
XLA Modules:
  0.0 108.4 jit_solution(12846636882807693981)
XLA Ops:
  0.6 102.9 %shard_map.103 = (f32[1,1]{1,0:T(1,128)}, bf16[128,1024]{1,0:T(8,128)(2,1)}, f32[64,256]{1,0:T(8,128)}) custom-call(bf16[128,1024]{1,0:T(8,128)(2,1)} %student.1, bf16[128,4096]{1,0:T(8,128)(2,1)} %teacher.1, f32[128,2048]{1,0:T(8,128)} %sims.1, bf16[1024,4096]{1,0:T(8,128)(2,1)} %projector.1, s32[2,128]{1,0:T(2,128)} %bitcast.5, s32[2,128]{1,0:T(2,128)} %bitcast.6, ...), custom_call_target="tpu_custom_call" | custom-call | flops 12000000000 | bytes 16000000 | tf_op jit(solution)/shard_map/pallas_call | solution.py:782
  104.1 1.7 %copy.15 = bf16[128,1024]{1,0:T(8,128)(2,1)} copy(bf16[128,1024]{1,0:T(8,128)(2,1)} %get-tuple-element.13) | data formatting | bytes 524288
  105.8 1.5 %copy.16 = f32[64,256]{1,0:T(8,128)} copy(f32[64,256]{1,0:T(8,128)} %get-tuple-element.14) | data formatting | bytes 131072
